TPU v7x, 512 devices: a whole 4x4x16 slice. The times are simulated.
512 devices in a mesh: seq: 64 (over x, z), ch: 8 (over y, core).
Axes of the slice: x: 4, y: 4, z: 16, core: 2. Of those that a mesh axis runs over, the one named last changes fastest.
Arguments:
- stream_one: bfloat16 [8192, 2048], P('seq', 'ch'), may hold values from -6 to 6
- stream_two: bfloat16 [8192, 2048], P('seq', 'ch'), may hold values from -6 to 6
- stream_value: bfloat16 [8192, 2048], P('seq', 'ch'), may hold values from -6 to 6
- long_filter: bfloat16 [8192, 2048], P('seq', 'ch'), may hold values from -4 to 4
- short_taps: float32 [3, 3, 2048], P(None, None, 'ch'), may hold values from -3.5 to 3.5
- skip_gain: float32 [2048], P('ch'), may hold values from -1 to 1
- out_grad: bfloat16 [8192, 2048], P('seq', 'ch'), may hold values from -0.59765625 to 0.59765625
Outputs:
- mixed_out: bfloat16 [8192, 2048], P('seq', 'ch')
- grad_one: bfloat16 [8192, 2048], P('seq', 'ch')
- grad_two: bfloat16 [8192, 2048], P('seq', 'ch')
- grad_value: bfloat16 [8192, 2048], P('seq', 'ch')
- grad_filter: float32 [8192, 2048], P('seq', 'ch')
- grad_taps: float32 [3, 3, 2048], P(None, None, 'ch')
- grad_skip: float32 [2048], P('ch')
All inputs are finite; a program needn't handle non-finite values.
Results may differ from a plain program's by a relative error of at most 0.0054.
Values may be sent and summed in bfloat16 or wider, within the bound.
A program may use at most 64 MiB of HBM per device.

v0:
```python
import math

import jax
import jax.numpy as jnp
from jax import lax
from jax.sharding import PartitionSpec as P

exact_mode = lax.Precision.HIGHEST


def passed_along(block, axis, distance):
    devices = range(lax.axis_size(axis))
    route = [(i - distance, i) for i in devices if i - distance in devices]
    return lax.ppermute(block, axis, route)


def swapped(array, axis, apart):
    return lax.ppermute(array, axis, [(i, i ^ 1 << apart) for i in range(lax.axis_size(axis))])


def unit_root(exponent, modulus):
    reduced = jnp.mod(exponent, modulus).astype(jnp.float32)
    phases = reduced * jnp.float32(-2.0 * math.pi / modulus)
    return (jnp.cos(phases), jnp.sin(phases))


def reverse_bits(values, sections):
    result = jnp.zeros_like(values)
    for bit_pos in range(sections):
        result = result + jnp.bitwise_and(jnp.right_shift(values, bit_pos), 1) * (
            1 << sections - 1 - bit_pos
        )
    return result


def rotate_pair(values, cosine, sine_part):
    shape_rest = values.shape[1:]
    flipped = values.reshape((2, 2) + shape_rest)[:, ::-1].reshape(values.shape)
    signs = jnp.array([-1.0, 1.0, -1.0, 1.0], jnp.float32).reshape((4,) + (1,) * len(shape_rest))
    return values * cosine + flipped * (signs * sine_part)


def lift_raw(raw_vals, dev_index, doubled):
    cosine, sine_part = unit_root(dev_index, doubled)
    return jnp.stack([raw_vals, jnp.zeros_like(raw_vals), raw_vals * cosine, raw_vals * sine_part])


def upper_flag(dev_index, bit_pos):
    return jnp.bitwise_and(jnp.right_shift(dev_index, bit_pos), 1) == 1


def forward_section(current, partner_vals, dev_index, bit_pos):
    half_span = 1 << bit_pos
    is_upper = upper_flag(dev_index, bit_pos)
    cosine, sine_part = unit_root(jnp.mod(dev_index, half_span), 2 * half_span)
    return jnp.where(
        is_upper, rotate_pair(partner_vals - current, cosine, sine_part), current + partner_vals
    )


def inverse_section(current, partner_vals, dev_index, bit_pos):
    half_span = 1 << bit_pos
    is_upper = upper_flag(dev_index, bit_pos)
    cosine, sine_part = unit_root(jnp.mod(dev_index, half_span), 2 * half_span)
    return jnp.where(
        is_upper,
        partner_vals - rotate_pair(current, cosine, -sine_part),
        current + rotate_pair(partner_vals, cosine, -sine_part),
    )


def fold_parities(current, exponent, doubled):
    cosine, sine_part = unit_root(exponent, doubled)
    real_part = current[0] + current[2] * cosine - current[3] * sine_part
    imag_part = current[1] + current[2] * sine_part + current[3] * cosine
    return (real_part, imag_part)


def settle_terms(current, dev_index, partner_index, bit_pos, doubled):
    half_span = 1 << bit_pos
    is_upper = upper_flag(dev_index, bit_pos)
    cosine, sine_part = unit_root(jnp.mod(dev_index, half_span), 2 * half_span)
    own_real, own_imag = fold_parities(current, -dev_index, doubled)
    peer_real, peer_imag = fold_parities(current, -partner_index, doubled)
    kept_part = jnp.where(is_upper, -(cosine * own_real + sine_part * own_imag), own_real)
    sent_part = jnp.where(is_upper, cosine * peer_real + sine_part * peer_imag, peer_real)
    return (kept_part, sent_part)


def spectral_tables(freq_slot, tokens, doubled):
    modulus = doubled * tokens
    freq_rows = jnp.arange(tokens, dtype=jnp.int32)[:, None]
    place_cols = jnp.arange(tokens, dtype=jnp.int32)[None, :]
    forward_list = []
    inverse_list = []
    for parity in range(2):
        global_freq = doubled * freq_rows + 2 * freq_slot + parity
        cosine, sine_part = unit_root(global_freq * place_cols, modulus)
        forward_list.append(
            jnp.concatenate(
                [jnp.concatenate([cosine, -sine_part], 1), jnp.concatenate([sine_part, cosine], 1)],
                0,
            )
        )
        inverse_list.append(
            jnp.concatenate(
                [
                    jnp.concatenate([cosine.T, sine_part.T], 1),
                    jnp.concatenate([-sine_part.T, cosine.T], 1),
                ],
                0,
            )
        )
    return (jnp.stack(forward_list), jnp.stack(inverse_list))


def per_device(stream_one, stream_two, stream_value, long_filter, short_taps, skip_gain, out_grad):
    devices = lax.axis_size("seq")
    sections = devices.bit_length() - 1
    top_bit = sections - 1
    dev_index = lax.axis_index("seq")
    partner_index = jnp.bitwise_xor(dev_index, 1 << top_bit)
    tokens = stream_one.shape[0]
    channels = stream_one.shape[1]
    doubled = 2 * devices
    modulus = doubled * tokens
    tap_count = short_taps.shape[1]
    streams = jnp.stack([stream_one, stream_two, stream_value])
    before = passed_along(streams[:, tokens - (tap_count - 1) :], "seq", 1)
    extended = jnp.concatenate([before, streams], axis=1).astype(jnp.float32)
    convolved = jnp.zeros(streams.shape, jnp.float32)
    for offset in range(tap_count):
        first_row = tap_count - 1 - offset
        convolved = (
            convolved + short_taps[:, offset, None, :] * extended[:, first_row : first_row + tokens]
        )
    gate_out, gate_in, value_conv = (convolved[0], convolved[1], convolved[2])
    cotangent = out_grad.astype(jnp.float32)
    mixed_in = lax.optimization_barrier((gate_in * value_conv).astype(jnp.bfloat16))
    back_grad = lax.optimization_barrier((cotangent * gate_out).astype(jnp.bfloat16))
    mixed_wide = mixed_in.astype(jnp.float32)
    back_wide = back_grad.astype(jnp.float32)
    raw_stack = jnp.stack([mixed_in, back_grad, long_filter], axis=1)
    freq_slot = reverse_bits(dev_index, sections)
    partner_raw = swapped(raw_stack, "seq", top_bit)
    current = forward_section(
        lift_raw(raw_stack.astype(jnp.float32), dev_index, doubled),
        lift_raw(partner_raw.astype(jnp.float32), partner_index, doubled),
        dev_index,
        top_bit,
    )
    for bit_pos in range(top_bit - 1, -1, -1):
        partner_vals = swapped(current, "seq", bit_pos)
        current = forward_section(current, partner_vals, dev_index, bit_pos)
    spectrum = current
    forward_tab, inverse_tab = spectral_tables(freq_slot, tokens, doubled)
    packed = spectrum.reshape(2, 2 * tokens, 3 * channels)
    spectral = jnp.einsum(
        "rkb,rbx->rkx",
        forward_tab,
        packed,
        precision=exact_mode,
        preferred_element_type=jnp.float32,
    )
    spectral = spectral.reshape(2, 2, tokens, 3, channels)
    mix_real, mix_imag = (spectral[:, 0, :, 0], spectral[:, 1, :, 0])
    back_real, back_imag = (spectral[:, 0, :, 1], spectral[:, 1, :, 1])
    filt_real, filt_imag = (spectral[:, 0, :, 2], spectral[:, 1, :, 2])
    conv_spec = jnp.stack(
        [mix_real * filt_real - mix_imag * filt_imag, mix_real * filt_imag + mix_imag * filt_real],
        1,
    )
    grad_mix_spec = jnp.stack(
        [
            back_real * filt_real + back_imag * filt_imag,
            back_imag * filt_real - back_real * filt_imag,
        ],
        1,
    )
    grad_filt_spec = jnp.stack(
        [back_real * mix_real + back_imag * mix_imag, back_imag * mix_real - back_real * mix_imag],
        1,
    )
    products = jnp.stack([conv_spec, grad_mix_spec, grad_filt_spec], axis=3).reshape(
        2, 2 * tokens, 3 * channels
    )
    returned = jnp.einsum(
        "rbk,rkx->rbx",
        inverse_tab,
        products,
        precision=exact_mode,
        preferred_element_type=jnp.float32,
    )
    returned = returned.reshape(4, tokens, 3, channels)
    current = returned
    for bit_pos in range(top_bit):
        partner_vals = swapped(current, "seq", bit_pos)
        current = inverse_section(current, partner_vals, dev_index, bit_pos)
    kept_part, sent_part = settle_terms(current, dev_index, partner_index, top_bit, doubled)
    circular = (kept_part + swapped(sent_part, "seq", top_bit)) * jnp.float32(1.0 / modulus)
    long_out = circular[:, 0] + skip_gain * mixed_wide
    mixed_out = (gate_out * long_out).astype(jnp.bfloat16)
    grad_mixed_in = circular[:, 1] + skip_gain * back_wide
    grad_filter = circular[:, 2]
    grad_skip_local = jnp.sum(back_wide * mixed_wide, axis=0)
    conv_grads = jnp.stack(
        [cotangent * long_out, grad_mixed_in * value_conv, grad_mixed_in * gate_in]
    )
    taps_list = []
    for offset in range(tap_count):
        first_row = tap_count - 1 - offset
        taps_list.append(jnp.sum(conv_grads * extended[:, first_row : first_row + tokens], axis=1))
    grad_taps_local = jnp.stack(taps_list, axis=1)
    next_rows = passed_along(conv_grads[:, : tap_count - 1], "seq", -1)
    trailing = jnp.concatenate([conv_grads, next_rows], axis=1)
    grad_streams = jnp.zeros_like(conv_grads)
    for offset in range(tap_count):
        grad_streams = (
            grad_streams + short_taps[:, offset, None, :] * trailing[:, offset : offset + tokens]
        )
    grad_streams = grad_streams.astype(jnp.bfloat16)
    grad_taps, grad_skip = lax.psum((grad_taps_local, grad_skip_local), "seq")
    return (
        mixed_out,
        grad_streams[0],
        grad_streams[1],
        grad_streams[2],
        grad_filter,
        grad_taps,
        grad_skip,
    )


def solution(mesh):
    in_specs = (
        P("seq", "ch"),
        P("seq", "ch"),
        P("seq", "ch"),
        P("seq", "ch"),
        P(None, None, "ch"),
        P("ch"),
        P("seq", "ch"),
    )
    out_specs = (
        P("seq", "ch"),
        P("seq", "ch"),
        P("seq", "ch"),
        P("seq", "ch"),
        P("seq", "ch"),
        P(None, None, "ch"),
        P("ch"),
    )
    return jax.shard_map(
        per_device, mesh=mesh, in_specs=in_specs, out_specs=out_specs, check_vma=False
    )
```

profile of v0, /device:TPU:24, one launch (start us, length us, event | category | flops | bytes accessed | tf_op | source)
XLA Modules:
  0.0 1269.1 jit_solution(1187683794862063340)
XLA Ops:
  1.4 3.8 collective-permute-start
  8.9 11.5 collective-permute-start.1
  20.6 3.9 collective-permute-done.1
  27.7 2.9 fusion.36
  30.5 3.6 collective-permute-start.2
  34.2 33.1 %collective-permute-done.2 = f32[4,128,3,256]{3,1,2,0:T(8,128)} collective-permute-done((f32[4,128,3,256]{3,1,2,0:T(8,128)}, f32[4,128,3,256]{3,1,2,0:T(8,128)}, u32[]{:S(2)}, u32[]{:S(2)}) %collective-permute-start.2) | collective-permute-done | bytes 1572896 | tf_op jit(solution)/shard_map/ppermute | solution.py:18
  67.3 3.5 fusion.104
  70.9 2.6 rev.49
  73.5 4.7 fusion.34
  78.2 8.8 collective-permute-start.3
  87.1 127.3 %collective-permute-done.3 = f32[4,128,3,256]{3,1,2,0:T(8,128)} collective-permute-done((f32[4,128,3,256]{3,1,2,0:T(8,128)}, f32[4,128,3,256]{3,1,2,0:T(8,128)}, u32[]{:S(2)}, u32[]{:S(2)}) %collective-permute-start.3) | collective-permute-done | bytes 1572896 | tf_op jit(solution)/shard_map/ppermute | solution.py:18
  217.8 4.1 fusion.32
  223.9 132.7 %collective-permute-done.4 = f32[4,128,3,256]{3,1,2,0:T(8,128)} collective-permute-done((f32[4,128,3,256]{3,1,2,0:T(8,128)}, f32[4,128,3,256]{3,1,2,0:T(8,128)}, u32[]{:S(2)}, u32[]{:S(2)}) %collective-permute-start.4) | collective-permute-done | bytes 1572896 | tf_op jit(solution)/shard_map/ppermute | solution.py:18
  360.1 4.1 fusion.30
  366.2 69.0 %collective-permute-done.5 = f32[4,128,3,256]{3,1,2,0:T(8,128)} collective-permute-done((f32[4,128,3,256]{3,1,2,0:T(8,128)}, f32[4,128,3,256]{3,1,2,0:T(8,128)}, u32[]{:S(2)}, u32[]{:S(2)}) %collective-permute-start.5) | collective-permute-done | bytes 1572896 | tf_op jit(solution)/shard_map/ppermute | solution.py:18
  438.7 4.1 fusion.28
  447.3 33.9 %collective-permute-done.6 = f32[4,128,3,256]{3,1,2,0:T(8,128)} collective-permute-done((f32[4,128,3,256]{3,1,2,0:T(8,128)}, f32[4,128,3,256]{3,1,2,0:T(8,128)}, u32[]{:S(2)}, u32[]{:S(2)}) %collective-permute-start.6) | collective-permute-done | bytes 1572896 | tf_op jit(solution)/shard_map/ppermute | solution.py:18
  484.7 2.9 fusion.26
  491.0 5.4 fusion.42
  508.4 2.5 reshape.582
  510.9 2.7 fusion.38
  513.6 2.6 reshape.583
  519.8 3.1 copy.123
  522.9 2.9 reshape_reshape.3
  525.8 8.8 rev.54
  534.7 3.7 copy.124
  538.3 16.9 %collective-permute-done.7 = f32[4,128,3,256]{3,1,2,0:T(8,128)} collective-permute-done((f32[4,128,3,256]{3,1,2,0:T(8,128)}, f32[4,128,3,256]{3,1,2,0:T(8,128)}, u32[]{:S(2)}, u32[]{:S(2)}) %collective-permute-start.7) | collective-permute-done | bytes 1572896 | tf_op jit(solution)/shard_map/ppermute | solution.py:18
  555.3 2.7 rev.55
  558.0 4.2 fusion.22
  562.2 2.3 collective-permute-start.8
  564.5 2.7 rev.56
  567.2 66.2 %collective-permute-done.8 = f32[4,128,3,256]{3,1,2,0:T(8,128)S(1)} collective-permute-done((f32[4,128,3,256]{3,1,2,0:T(8,128)}, f32[4,128,3,256]{3,1,2,0:T(8,128)S(1)}, u32[]{:S(2)}, u32[]{:S(2)}) %collective-permute-start.8) | collective-permute-done | bytes 1572896 | tf_op jit(solution)/shard_map/ppermute | solution.py:18
  635.1 3.5 fusion.17
  641.9 171.1 %collective-permute-done.9 = f32[4,128,3,256]{3,1,2,0:T(8,128)} collective-permute-done((f32[4,128,3,256]{3,1,2,0:T(8,128)S(1)}, f32[4,128,3,256]{3,1,2,0:T(8,128)}, u32[]{:S(2)}, u32[]{:S(2)}) %collective-permute-start.9) | collective-permute-done | bytes 1572896 | tf_op jit(solution)/shard_map/ppermute | solution.py:18
  813.0 2.7 rev.59
  815.7 4.3 fusion.12
  820.0 8.5 collective-permute-start.10
  828.4 2.7 rev.60
  831.2 53.8 %collective-permute-done.10 = f32[4,128,3,256]{3,1,2,0:T(8,128)S(1)} collective-permute-done((f32[4,128,3,256]{3,1,2,0:T(8,128)}, f32[4,128,3,256]{3,1,2,0:T(8,128)S(1)}, u32[]{:S(2)}, u32[]{:S(2)}) %collective-permute-start.10) | collective-permute-done | bytes 1572896 | tf_op jit(solution)/shard_map/ppermute | solution.py:18
  886.6 3.5 fusion.7
  890.1 3.6 collective-permute-start.11
  895.2 33.1 %collective-permute-done.11 = f32[4,128,3,256]{3,1,2,0:T(8,128)} collective-permute-done((f32[4,128,3,256]{3,1,2,0:T(8,128)S(1)}, f32[4,128,3,256]{3,1,2,0:T(8,128)}, u32[]{:S(2)}, u32[]{:S(2)}) %collective-permute-start.11) | collective-permute-done | bytes 1572896 | tf_op jit(solution)/shard_map/ppermute | solution.py:18
  928.3 2.7 rev.63
  931.0 3.5 fusion.2
  934.7 5.3 collective-permute-start.12
  940.1 8.2 collective-permute-done.12
  951.3 3.6 collective-permute-done.13
  955.2 312.7 %all-reduce = (f32[3,3,256]{2,0,1:T(4,128)S(1)}, f32[256]{0:T(256)}) all-reduce(f32[3,3,256]{2,0,1:T(4,128)S(1)} %pad_maximum_fusion.6, f32[256]{0:T(256)S(1)} %get-tuple-element.53), channel_id=1, replica_groups=mesh['seq'=64,'ch'=8] {'seq'}, use_global_device_ids=true, to_apply=%region_3.4 | all-reduce | flops 2560 | bytes 20480 | tf_op jit(solution)/shard_map/psum | solution.py:222
  (101 shorter events, 60.5 us)
Async XLA Ops:
  0.6 8.2 copy-start.11
  1.4 6.4 collective-permute-start
  5.2 3.7 copy-start.10
  8.8 15.7 %copy-start.6 = (f32[3,128,256]{2,1,0:T(8,128)}, f32[3,128,256]{2,1,0:T(8,128)S(1)}, u32[]{:S(2)}) copy-start(f32[3,128,256]{2,1,0:T(8,128)S(1)} %multiply_add_fusion) | copy-start | bytes 1179652
  8.9 15.5 %collective-permute-start.1 = (bf16[128,3,256]{2,0,1:T(8,128)(2,1)S(1)}, bf16[128,3,256]{2,0,1:T(8,128)(2,1)S(1)}, u32[]{:S(2)}, u32[]{:S(2)}) collective-permute-start(bf16[128,3,256]{2,0,1:T(8,128)(2,1)S(1)} %pad_maximum_fusion.5), channel_id=1, source_target_pairs={{0,256},{8,264},{16,272},{24,280},{32,288},{40,296},{48,304},{56,3... | collective-permute-start | bytes 589832 | tf_op jit(solution)/shard_map/ppermute | solution.py:18
  24.5 1.5 copy-start.1
  24.6 1.5 copy-start.2
  24.6 1.5 copy-start.3
  30.5 36.8 %collective-permute-start.2 = (f32[4,128,3,256]{3,1,2,0:T(8,128)}, f32[4,128,3,256]{3,1,2,0:T(8,128)}, u32[]{:S(2)}, u32[]{:S(2)}) collective-permute-start(f32[4,128,3,256]{3,1,2,0:T(8,128)} %fusion.36), channel_id=1, source_target_pairs={{0,128},{8,136},{16,144},{24,152},{32,160},{40,168},{48,176},{56,1... | collective-permute-start | bytes 4718600 | tf_op jit(solution)/shard_map/ppermute | solution.py:18
  78.2 136.2 %collective-permute-start.3 = (f32[4,128,3,256]{3,1,2,0:T(8,128)}, f32[4,128,3,256]{3,1,2,0:T(8,128)}, u32[]{:S(2)}, u32[]{:S(2)}) collective-permute-start(f32[4,128,3,256]{3,1,2,0:T(8,128)} %fusion.34), channel_id=1, source_target_pairs={{0,64},{8,72},{16,80},{24,88},{32,96},{40,104},{48,112},{56,120},{... | collective-permute-start | bytes 4718600 | tf_op jit(solution)/shard_map/ppermute | solution.py:18
  221.9 134.7 %collective-permute-start.4 = (f32[4,128,3,256]{3,1,2,0:T(8,128)}, f32[4,128,3,256]{3,1,2,0:T(8,128)}, u32[]{:S(2)}, u32[]{:S(2)}) collective-permute-start(f32[4,128,3,256]{3,1,2,0:T(8,128)} %fusion.32), channel_id=1, source_target_pairs={{0,32},{8,40},{16,48},{24,56},{32,0},{40,8},{48,16},{56,24},{64,96... | collective-permute-start | bytes 4718600 | tf_op jit(solution)/shard_map/ppermute | solution.py:18
  364.2 71.0 %collective-permute-start.5 = (f32[4,128,3,256]{3,1,2,0:T(8,128)}, f32[4,128,3,256]{3,1,2,0:T(8,128)}, u32[]{:S(2)}, u32[]{:S(2)}) collective-permute-start(f32[4,128,3,256]{3,1,2,0:T(8,128)} %fusion.30), channel_id=1, source_target_pairs={{0,16},{8,24},{16,0},{24,8},{32,48},{40,56},{48,32},{56,40},{64,80... | collective-permute-start | bytes 4718600 | tf_op jit(solution)/shard_map/ppermute | solution.py:18
  442.7 38.5 %collective-permute-start.6 = (f32[4,128,3,256]{3,1,2,0:T(8,128)}, f32[4,128,3,256]{3,1,2,0:T(8,128)}, u32[]{:S(2)}, u32[]{:S(2)}) collective-permute-start(f32[4,128,3,256]{3,1,2,0:T(8,128)} %fusion.28), channel_id=1, source_target_pairs={{0,8},{8,0},{16,24},{24,16},{32,40},{40,32},{48,56},{56,48},{64,72... | collective-permute-start | bytes 4718600 | tf_op jit(solution)/shard_map/ppermute | solution.py:18
  483.4 1.3 copy-start.14
  500.5 3.3 copy-start.8
  504.8 1.0 copy-start.9
  517.6 37.7 %collective-permute-start.7 = (f32[4,128,3,256]{3,1,2,0:T(8,128)}, f32[4,128,3,256]{3,1,2,0:T(8,128)}, u32[]{:S(2)}, u32[]{:S(2)}) collective-permute-start(f32[4,128,3,256]{3,1,2,0:T(8,128)} %copy.122), channel_id=1, source_target_pairs={{0,8},{8,0},{16,24},{24,16},{32,40},{40,32},{48,56},{56,48},{64,72... | collective-permute-start | bytes 4718600 | tf_op jit(solution)/shard_map/ppermute | solution.py:18
  555.3 2.7 copy-start.13
  562.2 71.2 %collective-permute-start.8 = (f32[4,128,3,256]{3,1,2,0:T(8,128)}, f32[4,128,3,256]{3,1,2,0:T(8,128)S(1)}, u32[]{:S(2)}, u32[]{:S(2)}) collective-permute-start(f32[4,128,3,256]{3,1,2,0:T(8,128)} %fusion.22), channel_id=1, source_target_pairs={{0,16},{8,24},{16,0},{24,8},{32,48},{40,56},{48,32},{56,40},{64,80... | collective-permute-start | bytes 4718600 | tf_op jit(solution)/shard_map/ppermute | solution.py:18
  633.4 1.7 copy-start.4
  638.6 174.4 %collective-permute-start.9 = (f32[4,128,3,256]{3,1,2,0:T(8,128)S(1)}, f32[4,128,3,256]{3,1,2,0:T(8,128)}, u32[]{:S(2)}, u32[]{:S(2)}) collective-permute-start(f32[4,128,3,256]{3,1,2,0:T(8,128)S(1)} %fusion.17), channel_id=1, source_target_pairs={{0,32},{8,40},{16,48},{24,56},{32,0},{40,8},{48,16},{56,24},{64,96... | collective-permute-start | bytes 4718600 | tf_op jit(solution)/shard_map/ppermute | solution.py:18
  820.0 65.0 %collective-permute-start.10 = (f32[4,128,3,256]{3,1,2,0:T(8,128)}, f32[4,128,3,256]{3,1,2,0:T(8,128)S(1)}, u32[]{:S(2)}, u32[]{:S(2)}) collective-permute-start(f32[4,128,3,256]{3,1,2,0:T(8,128)} %fusion.12), channel_id=1, source_target_pairs={{0,64},{8,72},{16,80},{24,88},{32,96},{40,104},{48,112},{56,120},{... | collective-permute-start | bytes 4718600 | tf_op jit(solution)/shard_map/ppermute | solution.py:18
  884.9 1.6 copy-start.5
  890.0 5.2 copy-start
  890.1 38.3 %collective-permute-start.11 = (f32[4,128,3,256]{3,1,2,0:T(8,128)S(1)}, f32[4,128,3,256]{3,1,2,0:T(8,128)}, u32[]{:S(2)}, u32[]{:S(2)}) collective-permute-start(f32[4,128,3,256]{3,1,2,0:T(8,128)S(1)} %fusion.7), channel_id=1, source_target_pairs={{0,128},{8,136},{16,144},{24,152},{32,160},{40,168},{48,176},{56,1... | collective-permute-start | bytes 4718600 | tf_op jit(solution)/shard_map/ppermute | solution.py:18
  934.6 13.9 %copy-start.7 = (f32[3,128,256]{2,1,0:T(8,128)S(1)}, f32[3,128,256]{2,1,0:T(8,128)}, u32[]{:S(2)}) copy-start(f32[3,128,256]{2,1,0:T(8,128)} %copy-done.6) | copy-start | bytes 1179652
  934.7 13.9 %copy-start.12 = (f32[256]{0:T(256)S(1)}, f32[256]{0:T(256)}, u32[]{:S(2)}) copy-start(f32[256]{0:T(256)} %param.28) | copy-start | bytes 3076
  934.7 13.7 %collective-permute-start.12 = (f32[128,3,256]{2,0,1:T(8,128)S(1)}, f32[128,3,256]{2,0,1:T(8,128)S(1)}, u32[]{:S(2)}, u32[]{:S(2)}) collective-permute-start(f32[128,3,256]{2,0,1:T(8,128)S(1)} %fusion.51), channel_id=1, source_target_pairs={{0,256},{8,264},{16,272},{24,280},{32,288},{40,296},{48,304},{56,3... | collective-permute-start | bytes 1179656 | tf_op jit(solution)/shard_map/ppermute | solution.py:18
  949.3 5.5 collective-permute-start.13
where the time goes:
time: 1270 us
  waiting for transfers between devices  753 us (59%)
  blocking collectives  313 us (25%)
  local copies, waits for them, and re-layouts  72 us (6%)
  other arithmetic  62.3 us (5%)
  starting transfers between devices  58.4 us (5%)
    ppermute x12, waiting for transfers between devices, swapped(): lax.ppermute(array, axis, [(i, i ^ 1 << apart) for i in range(lax.axis_si...  749 us
    psum x1, blocking collectives, per_device(): grad_taps, grad_skip = lax.psum((grad_taps_local, grad_skip_local), 'seq')  313 us
    ppermute x12, starting transfers between devices, swapped(): lax.ppermute(array, axis, [(i, i ^ 1 << apart) for i in range(lax.axis_si...  53.3 us
    rev x17, local copies, waits for them, and re-layouts, rotate_pair(): flipped = values.reshape((2, 2) + shape_rest)[:, ::-1].reshape(values.shape)  41.3 us
  transfers between devices with their start and end apart: 14, of which 13 were waited for; matrix products, arithmetic and copies ran while one was open for 2% of the time, Pallas kernels for 0%

commit v1 on v0

v1 whole, which is shorter than its diff:
```python
import functools
import math

import jax
import jax.numpy as jnp
import numpy as np
from jax import lax
from jax.experimental import pallas as pl
from jax.experimental.pallas import tpu as pltpu
from jax.sharding import PartitionSpec as P

MESH = pl.DeviceIdType.MESH
F32 = jnp.float32
BF16 = jnp.bfloat16


def halves(table):
    high = table.astype(BF16)
    low = (table - high.astype(np.float64)).astype(BF16)
    return high, low


def tables(devices, tokens, own):
    length = 2 * devices * tokens
    a = np.arange(devices)
    b = np.arange(tokens)
    odd = np.arange(devices) + 0.5
    outer = 2 * math.pi * np.outer(odd, a) / (2 * devices)
    first = np.concatenate([np.cos(outer), -np.sin(outer)], 0)
    last = np.concatenate([np.cos(outer.T), np.sin(outer.T)], 1) * (2.0 / length)
    turn = 2 * math.pi * np.outer(odd, b) / length
    inner = 2 * math.pi * (np.outer(b, b) % tokens) / tokens
    cosine, sine = np.cos(inner), np.sin(inner)
    second = np.block([[cosine, -sine], [sine, cosine]])
    order = np.zeros((own * devices, own * devices))
    for c in range(own):
        order[c * devices + a, a * own + c] = 1.0
    first_high, first_low = halves(first)
    return (
        np.concatenate([first_high, first_low], 0),
        np.stack(halves(last)),
        np.cos(turn).astype(np.float32),
        (-np.sin(turn)).astype(np.float32),
        np.stack(halves(second)),
        order.astype(BF16),
        order.T.astype(BF16),
    )


def split(x):
    high = x.astype(BF16)
    return high, (x - high.astype(F32)).astype(BF16)


def mul(a, b):
    return jnp.dot(a, b, preferred_element_type=F32)


def exchange_kernel(
    devices, own, one_ref, two_ref, value_ref, filter_ref, cot_ref, taps_ref, skip_ref,
    first_ref, last_ref, turn_re_ref, turn_im_ref, second_ref, order_ref, back_ref,
    out_ref, sums_ref,
    send, recv, ret, sums, send_sem, recv_sem, ret_sem, out_sem, sums_sems,
):
    me = lax.axis_index("seq")
    tokens = one_ref.shape[0]
    barrier = pltpu.get_barrier_semaphore()

    def greet(k, carry):
        pl.semaphore_signal(
            barrier, inc=1, device_id={"seq": lax.rem(me + k, devices)}, device_id_type=MESH
        )
        return carry

    lax.fori_loop(1, devices, greet, 0)

    sources = (filter_ref, two_ref, value_ref, one_ref, cot_ref)
    count = len(sources)

    def pack(p):
        send[p] = sources[p][...].T.reshape(devices, own, tokens)

    def spread(p, src, dst, ssem, rsem):
        def body(k, carry):
            d = lax.rem(me + k, devices)
            pltpu.make_async_remote_copy(
                src.at[p, d], dst.at[p, me], ssem.at[p], rsem.at[p],
                device_id={"seq": d}, device_id_type=MESH,
            ).start()
            return carry

        lax.fori_loop(1, devices, body, 0)
        pltpu.make_async_copy(src.at[p, me], dst.at[p, me], rsem.at[p]).start()

    for p in range(count):
        pack(p)
    pl.semaphore_wait(barrier, devices - 1)
    for p in range(count):
        spread(p, send, recv, send_sem, recv_sem)

    def arrive(p):
        pltpu.make_async_copy(recv.at[p], recv.at[p], recv_sem.at[p]).wait()
        got = mul(order_ref[...], recv[p].reshape(devices * own, tokens))
        return [got[c * devices : (c + 1) * devices] for c in range(own)]

    lane = lax.broadcasted_iota(jnp.int32, (devices, tokens), 1)
    row = lax.broadcasted_iota(jnp.int32, (devices, tokens), 0)

    def later(x, j):
        r = pltpu.roll(x, j, 1)
        up = jnp.where(row == 0, 0.0, pltpu.roll(r, 1, 0))
        return jnp.where(lane < j, up, r)

    def sooner(x, j):
        r = pltpu.roll(x, tokens - j, 1)
        down = jnp.where(row == devices - 1, 0.0, pltpu.roll(r, devices - 1, 0))
        return jnp.where(lane >= tokens - j, down, r)

    def tap(s, j, c):
        return taps_ref[3 * s + j, own * me + c]

    def short(s, c, x):
        moved = (x, later(x, 1), later(x, 2))
        total = tap(s, 0, c) * moved[0]
        total = total + tap(s, 1, c) * moved[1]
        return total + tap(s, 2, c) * moved[2], moved

    turn_re, turn_im = turn_re_ref[...], turn_im_ref[...]
    second_high, second_low = second_ref[0], second_ref[1]

    def rotate(re, im):
        return re * turn_re - im * turn_im, re * turn_im + im * turn_re

    def mul_second(x):
        high, low = split(x)
        return mul(high, second_high) + (mul(low, second_high) + mul(high, second_low))

    def forward(parts):
        rows = []
        for x in parts:
            both = mul(first_ref[...], x)
            both = both[: 2 * devices] + both[2 * devices :]
            rows.append(jnp.concatenate(rotate(both[:devices], both[devices:]), 1))
        full = mul_second(jnp.concatenate(rows, 0))
        return full[:, :tokens], full[:, tokens:]

    def inverse(re, im):
        full = mul_second(jnp.concatenate([re, im], 1))
        result = []
        for c in range(own):
            part = full[c * devices : (c + 1) * devices]
            high, low = split(jnp.concatenate(rotate(part[:, :tokens], part[:, tokens:]), 0))
            result.append(mul(last_ref[0], high) + (mul(last_ref[0], low) + mul(last_ref[1], high)))
        return result

    filt = [x.astype(BF16) for x in arrive(0)]
    filt_re, filt_im = forward(filt)
    two = [short(1, c, x) for c, x in enumerate(arrive(1))]
    val = [short(2, c, x) for c, x in enumerate(arrive(2))]
    mixed = [(two[c][0] * val[c][0]).astype(BF16) for c in range(own)]
    mix_re, mix_im = forward(mixed)
    conv = inverse(mix_re * filt_re - mix_im * filt_im, -(mix_re * filt_im + mix_im * filt_re))
    one = [short(0, c, x) for c, x in enumerate(arrive(3))]
    cot = arrive(4)
    back = [(cot[c] * one[c][0]).astype(BF16) for c in range(own)]
    back_re, back_im = forward(back)
    grad_filter = inverse(
        back_re * mix_re + back_im * mix_im, back_re * mix_im - back_im * mix_re
    )
    grad_mixed = inverse(
        back_re * filt_re + back_im * filt_im, back_re * filt_im - back_im * filt_re
    )

    def give(p, parts):
        stacked = jnp.concatenate([x.astype(BF16) for x in parts], 0)
        ret[p] = mul(back_ref[...], stacked).astype(BF16).reshape(devices, own, tokens)
        spread(p, ret, out_ref, ret_sem, out_sem)

    give(4, grad_filter)
    gathered = []
    outs = [[], [], [], []]
    for c in range(own):
        skip = skip_ref[0, own * me + c]
        mixed_wide, back_wide = mixed[c].astype(F32), back[c].astype(F32)
        long_out = conv[c] + skip * mixed_wide
        grad_in = grad_mixed[c] + skip * back_wide
        outs[0].append(one[c][0] * long_out)
        grads = (cot[c] * long_out, grad_in * val[c][0], grad_in * two[c][0])
        streams = (one[c][1], two[c][1], val[c][1])
        sections = []
        for s in range(3):
            total = tap(s, 0, c) * grads[s]
            total = total + tap(s, 1, c) * sooner(grads[s], 1)
            outs[1 + s].append(total + tap(s, 2, c) * sooner(grads[s], 2))
            for j in range(3):
                sections.append(grads[s] * streams[s][j])
        sections.append(back_wide * mixed_wide)
        for x in sections:
            gathered.append(x.reshape(devices // 8, 8, tokens).sum(0))
        for _ in range(6):
            gathered.append(jnp.zeros((8, tokens), F32))
    for p in range(4):
        give(p, outs[p])
    high, low = split(jnp.concatenate(gathered, 0))
    ones = jnp.ones((tokens, tokens), BF16)
    totals = mul(high, ones) + mul(low, ones)
    shape = totals.shape
    pick = lax.broadcasted_iota(jnp.int32, shape, 0) // 8 == lax.broadcasted_iota(jnp.int32, shape, 1)
    sums[...] = jnp.where(pick, totals, 0.0).sum(0, keepdims=True)

    def tell(k, carry):
        d = lax.rem(me + k, devices)
        pltpu.make_async_remote_copy(
            sums, sums_ref.at[me], sums_sems.at[0], sums_sems.at[1],
            device_id={"seq": d}, device_id_type=MESH,
        ).start()
        return carry

    lax.fori_loop(1, devices, tell, 0)
    pltpu.make_async_copy(sums, sums_ref.at[me], sums_sems.at[1]).start()

    others = pl.ds(0, devices - 1)
    for p in range(count):
        pltpu.make_async_copy(send.at[p, others], send.at[p, others], send_sem.at[p]).wait()
        pltpu.make_async_copy(ret.at[p, others], ret.at[p, others], ret_sem.at[p]).wait()
    for p in range(count):
        pltpu.make_async_copy(out_ref.at[p], out_ref.at[p], out_sem.at[p]).wait()
    pltpu.make_async_copy(sums_ref.at[others], sums_ref.at[others], sums_sems.at[0]).wait()
    pltpu.make_async_copy(sums_ref, sums_ref, sums_sems.at[1]).wait()


def finish_kernel(
    got_ref, sums_ref, mixed_out_ref, one_ref, two_ref, value_ref, filter_ref, taps_ref, skip_ref
):
    _, devices, own, tokens = got_ref.shape
    for p, ref in enumerate((mixed_out_ref, one_ref, two_ref, value_ref, filter_ref)):
        ref[...] = got_ref[p].reshape(devices * own, tokens).T.astype(ref.dtype)
    turned = sums_ref[...].reshape(devices, tokens).T
    source = lax.broadcasted_iota(jnp.int32, (devices, devices * own), 0)
    target = lax.broadcasted_iota(jnp.int32, (devices, devices * own), 1)
    total = jnp.zeros((16, devices * own), F32)
    for c in range(own):
        place = jnp.where(target == source * own + c, 1.0, 0.0)
        total = total + jnp.dot(
            turned[16 * c : 16 * (c + 1)], place,
            precision=lax.Precision.HIGHEST, preferred_element_type=F32,
        )
    taps_ref[...] = total[:9]
    skip_ref[...] = total[9:10]


def per_device(one, two, value, long_filter, short_taps, skip_gain, out_grad):
    devices = lax.axis_size("seq")
    tokens, channels = one.shape
    own = channels // devices
    vmem = pl.BlockSpec(memory_space=pltpu.VMEM)
    smem = pl.BlockSpec(memory_space=pltpu.SMEM)
    consts = [jnp.asarray(t) for t in tables(devices, tokens, own)]
    blocks = (5, devices, own, tokens)
    got, sums = pl.pallas_call(
        functools.partial(exchange_kernel, devices, own),
        out_shape=(
            jax.ShapeDtypeStruct(blocks, BF16),
            jax.ShapeDtypeStruct((devices, 1, tokens), F32),
        ),
        in_specs=[vmem] * 5 + [smem] * 2 + [vmem] * len(consts),
        out_specs=(vmem, vmem),
        scratch_shapes=[
            pltpu.VMEM(blocks, BF16),
            pltpu.VMEM(blocks, BF16),
            pltpu.VMEM(blocks, BF16),
            pltpu.VMEM((1, tokens), F32),
            pltpu.SemaphoreType.DMA((5,)),
            pltpu.SemaphoreType.DMA((5,)),
            pltpu.SemaphoreType.DMA((5,)),
            pltpu.SemaphoreType.DMA((5,)),
            pltpu.SemaphoreType.DMA((2,)),
        ],
        compiler_params=pltpu.CompilerParams(
            collective_id=0, has_side_effects=True, vmem_limit_bytes=40 * 1024 * 1024
        ),
        name="exchange",
    )(
        one, two, value, long_filter, out_grad,
        short_taps.reshape(9, channels), skip_gain.reshape(1, channels), *consts,
    )
    full = jax.ShapeDtypeStruct((tokens, channels), BF16)
    *outs, taps, skip = pl.pallas_call(
        finish_kernel,
        out_shape=(
            full, full, full, full,
            jax.ShapeDtypeStruct((tokens, channels), F32),
            jax.ShapeDtypeStruct((9, channels), F32),
            jax.ShapeDtypeStruct((1, channels), F32),
        ),
        in_specs=[vmem] * 2,
        out_specs=(vmem,) * 7,
        name="finish",
    )(got, sums)
    return (*outs, taps.reshape(3, 3, channels), skip.reshape(channels))


def solution(mesh):
    rows, lanes = P("seq", "ch"), P("ch")
    taps = P(None, None, "ch")
    return jax.shard_map(
        per_device,
        mesh=mesh,
        in_specs=(rows, rows, rows, rows, taps, lanes, rows),
        out_specs=(rows, rows, rows, rows, rows, taps, lanes),
        check_vma=False,
    )
```

time: 1270 us -> 76 us (0.06)
  waiting for transfers between devices: 753 us -> 0 us
  blocking collectives: 313 us -> 0 us
  other arithmetic: 62.3 us -> 0 us
  Pallas kernels: 0 us -> 61.9 us
  local copies, waits for them, and re-layouts: 72 us -> 12.7 us
  starting transfers between devices: 58.4 us -> 0 us
    ppermute x14 -> x0, waiting for transfers between devices: 753 us -> none  [the longest x12 749 us: swapped(): lax.ppermute(array, axis, [(i, i ^ 1 << apart) for i in range(lax.axis_si...]
    psum x1 -> x0, blocking collectives: 313 us -> none  [per_device(): grad_taps, grad_skip = lax.psum((grad_taps_local, grad_skip_local), 'seq')]
    pallas_call x0 -> x2, Pallas kernels: none -> 61.9 us  [the longest x1 60 us: per_device(): pl.pallas_call(functools.partial(exchange_kernel, devices, own), out_shap...]
    ppermute x14 -> x0, starting transfers between devices: 58.4 us -> none  [the longest x12 53.3 us: swapped(): lax.ppermute(array, axis, [(i, i ^ 1 << apart) for i in range(lax.axis_si...]
    select_n x12 -> x0, other arithmetic: 41.7 us -> none  [the longest x6 22.7 us: forward_section(): jnp.where(is_upper, rotate_pair(partner_vals - current, cosine, sine_part...]
    rev x17 -> x0, local copies, waits for them, and re-layouts: 41.3 us -> none  [rotate_pair(): flipped = values.reshape((2, 2) + shape_rest)[:, ::-1].reshape(values.shape)]
    sub x8 -> x0, other arithmetic: 13.7 us -> none  [the longest x6 13.5 us: forward_section(): partner_vals - current]
  transfers between devices with their start and end apart: 14 -> 0, of which waited for: 13 -> 0; matrix products, arithmetic and copies ran while one was open for 2% -> 0% of each run, Pallas kernels for 0% -> 0%
where the time goes in v1:
time: 76 us; the launch traced here: 75.3 us
  Pallas kernels  61.9 us (81%)
  local copies, waits for them, and re-layouts  12.7 us (17%)
    pallas_call x1, Pallas kernels, per_device(): pl.pallas_call(functools.partial(exchange_kernel, devices, own), out_shap...  60 us
    unnamed x30, local copies, waits for them, and re-layouts  10.7 us
    pallas_call x1, Pallas kernels, per_device(): pl.pallas_call(finish_kernel, out_shape=(full, full, full, full, jax.Shap...  1.91 us

profile of v1, /device:TPU:24, one launch (start us, length us, event | category | flops | bytes accessed | tf_op | source)
XLA Modules:
  0.0 75.3 jit_solution(2796114673406379543)
XLA Ops:
  0.6 0.0 copy-start.10
  0.6 0.0 copy-start.14
  0.7 0.7 reshape.26.taps_ref
  1.4 0.0 copy-done.10
  1.4 0.0 copy-done.14
  1.4 0.0 copy-start.1
  1.4 0.9 %copy-done.1 = bf16[2,256,256]{2,1,0:T(8,128)(2,1)S(1)} copy-done((bf16[2,256,256]{2,1,0:T(8,128)(2,1)S(1)}, bf16[2,256,256]{2,1,0:T(8,128)(2,1)}, u32[]{:S(2)}) %copy-start.1) | copy-done | bytes 262168
  2.3 0.0 copy-start.2
  2.4 0.9 %copy-done.2 = bf16[256,256]{1,0:T(8,128)(2,1)S(1)} copy-done((bf16[256,256]{1,0:T(8,128)(2,1)S(1)}, bf16[256,256]{1,0:T(8,128)(2,1)}, u32[]{:S(2)}) %copy-start.2) | copy-done | bytes 131096
  3.3 0.0 copy-start.3
  3.3 0.9 %copy-done.3 = bf16[256,256]{1,0:T(8,128)(2,1)S(1)} copy-done((bf16[256,256]{1,0:T(8,128)(2,1)S(1)}, bf16[256,256]{1,0:T(8,128)(2,1)}, u32[]{:S(2)}) %copy-start.3) | copy-done | bytes 131096
  4.2 0.0 copy-start.4
  4.2 0.8 %copy-done.4 = bf16[128,256]{1,0:T(8,128)(2,1)S(1)} copy-done((bf16[128,256]{1,0:T(8,128)(2,1)S(1)}, bf16[128,256]{1,0:T(8,128)(2,1)}, u32[]{:S(2)}) %copy-start.4) | copy-done | bytes 65560
  5.0 0.0 copy-start.5
  5.0 0.8 %copy-done.5 = bf16[128,256]{1,0:T(8,128)(2,1)S(1)} copy-done((bf16[128,256]{1,0:T(8,128)(2,1)S(1)}, bf16[128,256]{1,0:T(8,128)(2,1)}, u32[]{:S(2)}) %copy-start.5) | copy-done | bytes 65560
  5.8 0.0 copy-start.6
  5.8 0.8 %copy-done.6 = bf16[128,256]{1,0:T(8,128)(2,1)S(1)} copy-done((bf16[128,256]{1,0:T(8,128)(2,1)S(1)}, bf16[128,256]{1,0:T(8,128)(2,1)}, u32[]{:S(2)}) %copy-start.6) | copy-done | bytes 65560
  6.7 0.0 copy-start.7
  6.7 0.8 %copy-done.7 = bf16[128,256]{1,0:T(8,128)(2,1)S(1)} copy-done((bf16[128,256]{1,0:T(8,128)(2,1)S(1)}, bf16[128,256]{1,0:T(8,128)(2,1)}, u32[]{:S(2)}) %copy-start.7) | copy-done | bytes 65560
  7.5 0.0 copy-start.8
  7.5 0.8 %copy-done.8 = bf16[128,256]{1,0:T(8,128)(2,1)S(1)} copy-done((bf16[128,256]{1,0:T(8,128)(2,1)S(1)}, bf16[128,256]{1,0:T(8,128)(2,1)}, u32[]{:S(2)}) %copy-start.8) | copy-done | bytes 65560
  8.4 0.0 copy-start.9
  8.4 0.8 %copy-done.9 = bf16[256,64]{1,0:T(8,128)(2,1)S(1)} copy-done((bf16[256,64]{1,0:T(8,128)(2,1)S(1)}, bf16[256,64]{1,0:T(8,128)(2,1)}, u32[]{:S(2)}) %copy-start.9) | copy-done | bytes 32792
  9.2 0.0 copy-start.11
  9.2 0.8 %copy-done.11 = f32[64,128]{1,0:T(8,128)S(1)} copy-done((f32[64,128]{1,0:T(8,128)S(1)}, f32[64,128]{1,0:T(8,128)}, u32[]{:S(2)}) %copy-start.11) | copy-done | bytes 32792
  10.0 0.0 copy-start.12
  10.0 0.8 %copy-done.12 = bf16[2,64,128]{2,1,0:T(8,128)(2,1)S(1)} copy-done((bf16[2,64,128]{2,1,0:T(8,128)(2,1)S(1)}, bf16[2,64,128]{2,1,0:T(8,128)(2,1)}, u32[]{:S(2)}) %copy-start.12) | copy-done | bytes 32792
  10.7 60.0 %exchange.1 = (bf16[5,64,4,128]{3,2,1,0:T(4,128)(2,1)S(1)}, f32[64,1,128]{2,1,0:T(1,128)S(1)}) custom-call(bf16[128,256]{1,0:T(8,128)(2,1)S(1)} %copy-done.4, bf16[128,256]{1,0:T(8,128)(2,1)S(1)} %copy-done.5, bf16[128,256]{1,0:T(8,128)(2,1)S(1)} %copy-done.6, bf16[128,256]{1,0:T(8,128)(2,1)S(1)} %copy-done.7, bf16[128,256]{1,0:T(8,128)(2,1)S(1)} %copy-done.8, ...), custom_call_target="tpu_custom_call" | custom-call | tf_op jit(solution)/shard_map/exchange/pallas_call | solution.py:260
  70.7 0.0 copy-start
  70.7 0.7 copy-done
  71.5 0.0 copy-start.13
  71.5 0.6 copy-done.13
  72.1 1.9 %finish.1 = (bf16[128,256]{1,0:T(8,128)(2,1)}, bf16[128,256]{1,0:T(8,128)(2,1)}, bf16[128,256]{1,0:T(8,128)(2,1)}, bf16[128,256]{1,0:T(8,128)(2,1)}, f32[128,256...) custom-call(bf16[5,64,4,128]{3,2,1,0:T(4,128)(2,1)} %copy-done, f32[64,1,128]{2,1,0:T(1,128)} %copy-done.13), custom_call_target="tpu_custom_call" | custom-call | tf_op jit(solution)/shard_map/finish/pallas_call | solution.py:288
  74.0 1.3 %reshape.28 = f32[3,3,256]{2,1,0:T(4,128)} reshape(f32[9,256]{1,0:T(8,128)} %get-tuple-element.23) | data formatting | bytes 18432 | tf_op jit(solution)/shard_map/reshape | solution.py:300
Async XLA Ops:
  0.6 0.8 %copy-start.10 = (f32[64,128]{1,0:T(8,128)S(1)}, f32[64,128]{1,0:T(8,128)}, u32[]{:S(2)}) copy-start(f32[64,128]{1,0:T(8,128)} %constant.17.clone.turn_im_ref) | copy-start | bytes 98308
  0.6 0.8 copy-start.14
  1.4 1.0 %copy-start.1 = (bf16[2,256,256]{2,1,0:T(8,128)(2,1)S(1)}, bf16[2,256,256]{2,1,0:T(8,128)(2,1)}, u32[]{:S(2)}) copy-start(bf16[2,256,256]{2,1,0:T(8,128)(2,1)} %constant.18.clone.second_ref) | copy-start | bytes 786436
  2.3 0.9 %copy-start.2 = (bf16[256,256]{1,0:T(8,128)(2,1)S(1)}, bf16[256,256]{1,0:T(8,128)(2,1)}, u32[]{:S(2)}) copy-start(bf16[256,256]{1,0:T(8,128)(2,1)} %constant.20.clone.back_ref) | copy-start | bytes 393220
  3.3 0.9 %copy-start.3 = (bf16[256,256]{1,0:T(8,128)(2,1)S(1)}, bf16[256,256]{1,0:T(8,128)(2,1)}, u32[]{:S(2)}) copy-start(bf16[256,256]{1,0:T(8,128)(2,1)} %constant.19.clone.order_ref) | copy-start | bytes 393220
  4.2 0.8 %copy-start.4 = (bf16[128,256]{1,0:T(8,128)(2,1)S(1)}, bf16[128,256]{1,0:T(8,128)(2,1)}, u32[]{:S(2)}) copy-start(bf16[128,256]{1,0:T(8,128)(2,1)} %one_ref.1) | copy-start | bytes 196612
  5.0 0.8 %copy-start.5 = (bf16[128,256]{1,0:T(8,128)(2,1)S(1)}, bf16[128,256]{1,0:T(8,128)(2,1)}, u32[]{:S(2)}) copy-start(bf16[128,256]{1,0:T(8,128)(2,1)} %two_ref.1) | copy-start | bytes 196612
  5.8 0.8 %copy-start.6 = (bf16[128,256]{1,0:T(8,128)(2,1)S(1)}, bf16[128,256]{1,0:T(8,128)(2,1)}, u32[]{:S(2)}) copy-start(bf16[128,256]{1,0:T(8,128)(2,1)} %value_ref.1) | copy-start | bytes 196612
  6.7 0.8 %copy-start.7 = (bf16[128,256]{1,0:T(8,128)(2,1)S(1)}, bf16[128,256]{1,0:T(8,128)(2,1)}, u32[]{:S(2)}) copy-start(bf16[128,256]{1,0:T(8,128)(2,1)} %filter_ref.1) | copy-start | bytes 196612
  7.5 0.8 %copy-start.8 = (bf16[128,256]{1,0:T(8,128)(2,1)S(1)}, bf16[128,256]{1,0:T(8,128)(2,1)}, u32[]{:S(2)}) copy-start(bf16[128,256]{1,0:T(8,128)(2,1)} %cot_ref.1) | copy-start | bytes 196612
  8.4 0.8 %copy-start.9 = (bf16[256,64]{1,0:T(8,128)(2,1)S(1)}, bf16[256,64]{1,0:T(8,128)(2,1)}, u32[]{:S(2)}) copy-start(bf16[256,64]{1,0:T(8,128)(2,1)} %constant.14.clone.first_ref) | copy-start | bytes 98308
  9.2 0.8 %copy-start.11 = (f32[64,128]{1,0:T(8,128)S(1)}, f32[64,128]{1,0:T(8,128)}, u32[]{:S(2)}) copy-start(f32[64,128]{1,0:T(8,128)} %constant.16.clone.turn_re_ref) | copy-start | bytes 98308
  10.0 0.8 %copy-start.12 = (bf16[2,64,128]{2,1,0:T(8,128)(2,1)S(1)}, bf16[2,64,128]{2,1,0:T(8,128)(2,1)}, u32[]{:S(2)}) copy-start(bf16[2,64,128]{2,1,0:T(8,128)(2,1)} %constant.15.clone.last_ref) | copy-start | bytes 98308
  70.7 0.7 copy-start
  71.5 0.6 copy-start.13

commit v2 on v1

v2 whole, which is shorter than its diff:
```python
import functools
import math

import jax
import jax.numpy as jnp
import numpy as np
from jax import lax
from jax.experimental import pallas as pl
from jax.experimental.pallas import tpu as pltpu
from jax.sharding import PartitionSpec as P

MESH = pl.DeviceIdType.MESH
F32 = jnp.float32
BF16 = jnp.bfloat16
LANES = 128
HALO_LATER, HALO_SOONER, SUMS, FIELD = 0, 6, 12, 32


def halves(table):
    high = table.astype(BF16)
    low = (table - high.astype(np.float64)).astype(BF16)
    return high, low


def tables(devices, tokens, own):
    length = 2 * devices * tokens
    a = np.arange(devices)
    b = np.arange(tokens)
    odd = np.arange(devices) + 0.5
    outer = 2 * math.pi * np.outer(odd, a) / (2 * devices)
    first = np.concatenate([np.cos(outer), -np.sin(outer)], 0)
    last = np.concatenate([np.cos(outer.T), np.sin(outer.T)], 1) * (2.0 / length)
    turn = 2 * math.pi * np.outer(odd, b) / length
    inner = 2 * math.pi * (np.outer(b, b) % tokens) / tokens
    cosine, sine = np.cos(inner), np.sin(inner)
    second = np.block([[cosine, -sine], [sine, cosine]])
    order = np.zeros((own * devices, own * devices))
    for c in range(own):
        order[c * devices + a, a * own + c] = 1.0
    return (
        np.concatenate(halves(first), 0),
        np.stack(halves(last)),
        np.stack([np.cos(turn), -np.sin(turn)]).astype(np.float32),
        np.stack(halves(second)),
        np.stack([order, order.T]).astype(BF16),
    )


def split(x):
    high = x.astype(BF16)
    return high, (x - high.astype(F32)).astype(BF16)


def mul(a, b):
    return jnp.dot(a, b, preferred_element_type=F32)


def exchange_kernel(
    devices, parts, own,
    filter_in, two_in, value_in, one_in, cot_in, first_in, last_in, turn_in, second_in, order_in,
    taps_ref, skip_ref,
    out_ref, edge_ref,
    filter_ref, two_ref, value_ref, one_ref, cot_ref,
    first_ref, last_ref, turn_ref, second_ref, order_ref,
    send, recv, ret, edge,
    load_sem, send_sem, recv_sem, ret_sem, out_sem, edge_sem,
):
    me = lax.axis_index("seq")
    tokens = filter_ref.shape[0]
    barrier = pltpu.get_barrier_semaphore()
    inputs = (filter_in, two_in, value_in, one_in, cot_in, first_in, last_in, turn_in, second_in, order_in)
    held = (filter_ref, two_ref, value_ref, one_ref, cot_ref, first_ref, last_ref, turn_ref, second_ref, order_ref)
    loads = [pltpu.make_async_copy(x, y, load_sem.at[i]) for i, (x, y) in enumerate(zip(inputs, held))]
    for load in loads:
        load.start()

    def greet(k, carry):
        pl.semaphore_signal(
            barrier, inc=1, device_id={"seq": lax.rem(me + k, devices)}, device_id_type=MESH
        )
        return carry

    lax.fori_loop(1, devices, greet, 0)

    def spread(src, dst, ssem, rsem):
        def body(k, carry):
            d = lax.rem(me + k, devices)
            pltpu.make_async_remote_copy(
                src.at[d], dst.at[me], ssem, rsem, device_id={"seq": d}, device_id_type=MESH
            ).start()
            return carry

        lax.fori_loop(1, devices, body, 0)
        pltpu.make_async_copy(src.at[me], dst.at[me], rsem).start()

    for p in range(5):
        loads[p].wait()
        for h in range(parts):
            block = held[p][:, h * LANES : (h + 1) * LANES].T
            send[h, :, p] = block.reshape(devices, own, tokens)
    pl.semaphore_wait(barrier, devices - 1)
    for h in range(parts):
        spread(send.at[h], recv.at[h], send_sem.at[h], recv_sem.at[h])
    for load in loads[5:]:
        load.wait()

    lane = lax.broadcasted_iota(jnp.int32, (devices, tokens), 1)
    row = lax.broadcasted_iota(jnp.int32, (devices, tokens), 0)

    def later(x, j):
        r = pltpu.roll(x, j, 1)
        up = jnp.where(row == 0, 0.0, pltpu.roll(r, 1, 0))
        return jnp.where(lane < j, up, r)

    def tap(s, j, channel):
        return taps_ref[s, j, channel]

    def short(s, channel, x):
        moved = (x, later(x, 1), later(x, 2))
        total = tap(s, 0, channel) * moved[0]
        total = total + tap(s, 1, channel) * moved[1]
        return total + tap(s, 2, channel) * moved[2], moved

    turn_re, turn_im = turn_ref[0], turn_ref[1]

    def rotate(re, im):
        return re * turn_re - im * turn_im, re * turn_im + im * turn_re

    def mul_second(x):
        high, low = split(x)
        return mul(high, second_ref[0]) + (mul(low, second_ref[0]) + mul(high, second_ref[1]))

    def rows_of(x, i):
        return x[i * devices : (i + 1) * devices]

    def forward(pieces):
        rows = []
        for x in pieces:
            both = mul(first_ref[...], x)
            both = both[: 2 * devices] + both[2 * devices :]
            rows.append(jnp.concatenate(rotate(both[:devices], both[devices:]), 1))
        full = mul_second(jnp.concatenate(rows, 0))
        size = own * devices
        return [
            (full[i * size : (i + 1) * size, :tokens], full[i * size : (i + 1) * size, tokens:])
            for i in range(len(pieces) // own)
        ]

    def inverse(spectra):
        full = mul_second(jnp.concatenate([jnp.concatenate(z, 1) for z in spectra], 0))
        result = []
        for i in range(len(spectra) * own):
            part = rows_of(full, i)
            high, low = split(jnp.concatenate(rotate(part[:, :tokens], part[:, tokens:]), 0))
            result.append(mul(last_ref[0], high) + (mul(last_ref[0], low) + mul(last_ref[1], high)))
        return [result[i * own : (i + 1) * own] for i in range(len(spectra))]

    edges = jnp.zeros((devices, tokens), F32)
    sums = jnp.zeros((1, tokens), F32)
    ones = jnp.ones((tokens, tokens), BF16)
    for h in range(parts):
        pltpu.make_async_copy(recv.at[h], recv.at[h], recv_sem.at[h]).wait()
        got = []
        for p in range(5):
            x = mul(order_ref[0], recv[h, :, p].reshape(devices * own, tokens))
            got.append([rows_of(x, c) for c in range(own)])
        channels = [h * LANES + own * me + c for c in range(own)]
        filt = [x.astype(BF16) for x in got[0]]
        two = [short(1, channels[c], got[1][c]) for c in range(own)]
        val = [short(2, channels[c], got[2][c]) for c in range(own)]
        one = [short(0, channels[c], got[3][c]) for c in range(own)]
        cot = got[4]
        mixed = [(two[c][0] * val[c][0]).astype(BF16) for c in range(own)]
        back = [(cot[c] * one[c][0]).astype(BF16) for c in range(own)]
        (f_re, f_im), (m_re, m_im), (b_re, b_im) = forward(filt + mixed + back)
        conv, grad_mixed, grad_filter = inverse([
            (m_re * f_re - m_im * f_im, -(m_re * f_im + m_im * f_re)),
            (b_re * f_re + b_im * f_im, b_re * f_im - b_im * f_re),
            (b_re * m_re + b_im * m_im, b_re * m_im - b_im * m_re),
        ])
        wide = []
        for c in range(own):
            skip = skip_ref[channels[c]]
            mixed_wide, back_wide = mixed[c].astype(F32), back[c].astype(F32)
            wide.append((mixed_wide, back_wide, conv[c] + skip * mixed_wide, grad_mixed[c] + skip * back_wide))
        for p, pieces in enumerate(([w[2] for w in wide], [w[3] for w in wide], grad_filter)):
            stacked = jnp.concatenate([x.astype(BF16) for x in pieces], 0)
            ret[h, :, p] = mul(order_ref[1], stacked).astype(BF16).reshape(devices, own, tokens)
        spread(ret.at[h], out_ref.at[h], ret_sem.at[h], out_sem.at[h])

        sections = []
        for c in range(own):
            mixed_wide, back_wide, long_out, grad_in = wide[c]
            grads = (cot[c] * long_out, grad_in * val[c][0], grad_in * two[c][0])
            streams = (one[c][1], two[c][1], val[c][1])
            start = FIELD * (h * own + c)
            for s in range(3):
                at = start + HALO_LATER + 2 * s
                piece = pltpu.roll(streams[s][2], at, 1) if at else streams[s][2]
                edges = jnp.where((lane >= at) & (lane < at + 2), piece, edges)
                at = start + HALO_SOONER + 2 * s
                ahead = jnp.where(row == devices - 1, 0.0, pltpu.roll(grads[s], devices - 1, 0))
                edges = jnp.where((lane >= at) & (lane < at + 2), pltpu.roll(ahead, at, 1), edges)
                for j in range(3):
                    sections.append(grads[s] * streams[s][j])
            sections.append(back_wide * mixed_wide)
            sections += [None] * 6
        gathered = [
            jnp.zeros((8, tokens), F32) if x is None else x.reshape(devices // 8, 8, tokens).sum(0)
            for x in sections
        ]
        high, low = split(jnp.concatenate(gathered, 0))
        totals = mul(high, ones) + mul(low, ones)
        section = lax.broadcasted_iota(jnp.int32, totals.shape, 0) // 8
        target = FIELD * (h * own + section // 16) + SUMS + section % 16
        pick = lax.broadcasted_iota(jnp.int32, totals.shape, 1) == target
        sums = sums + jnp.where(pick, totals, 0.0).sum(0, keepdims=True)

    edge[...] = (edges + sums).reshape(devices, 1, tokens)
    spread(edge, edge_ref, edge_sem.at[0], edge_sem.at[1])

    others = pl.ds(0, devices - 1)

    def settle(ref, sem):
        pltpu.make_async_copy(ref, ref, sem).wait()

    for h in range(parts):
        settle(send.at[h, others], send_sem.at[h])
        settle(ret.at[h, others], ret_sem.at[h])
        settle(out_ref.at[h], out_sem.at[h])
    settle(edge.at[others], edge_sem.at[0])
    settle(edge_ref, edge_sem.at[1])


def finish_kernel(
    got_ref, edge_ref, one_ref, two_ref, value_ref, cot_ref, taps_ref,
    mixed_out_ref, grad_one_ref, grad_two_ref, grad_value_ref, filter_ref, taps_out_ref, skip_out_ref,
):
    parts, devices, _, own, tokens = got_ref.shape
    turned = edge_ref[...].reshape(devices, tokens).T
    source = lax.broadcasted_iota(jnp.int32, (devices, LANES), 0)
    target = lax.broadcasted_iota(jnp.int32, (devices, LANES), 1)
    row = lax.broadcasted_iota(jnp.int32, (tokens, LANES), 0)
    for h in range(parts):
        at = slice(h * LANES, (h + 1) * LANES)
        edges = jnp.zeros((FIELD, LANES), F32)
        for c in range(own):
            place = jnp.where(target == source * own + c, 1.0, 0.0)
            start = FIELD * (h * own + c)
            edges = edges + jnp.dot(
                turned[start : start + FIELD], place,
                precision=lax.Precision.HIGHEST, preferred_element_type=F32,
            )

        def edge(i):
            return edges[i : i + 1]

        def tap(s, j):
            return taps_ref[s, j : j + 1, at]

        long_out, grad_in, grad_filter = [
            got_ref[h, :, p].reshape(LANES, tokens).T.astype(F32) for p in range(3)
        ]
        gates = []
        for s, ref in enumerate((one_ref, two_ref, value_ref)):
            x = ref[:, at].astype(F32)
            i = HALO_LATER + 2 * s
            once = jnp.where(row == 0, edge(i + 1), pltpu.roll(x, 1, 0))
            twice = jnp.where(row == 0, edge(i), jnp.where(row == 1, edge(i + 1), pltpu.roll(x, 2, 0)))
            total = tap(s, 0) * x
            total = total + tap(s, 1) * once
            gates.append(total + tap(s, 2) * twice)
        mixed_out_ref[:, at] = (gates[0] * long_out).astype(BF16)
        grads = (cot_ref[:, at].astype(F32) * long_out, grad_in * gates[2], grad_in * gates[1])
        for s, ref in enumerate((grad_one_ref, grad_two_ref, grad_value_ref)):
            x = grads[s]
            i = HALO_SOONER + 2 * s
            once = jnp.where(row == tokens - 1, edge(i), pltpu.roll(x, tokens - 1, 0))
            twice = pltpu.roll(x, tokens - 2, 0)
            twice = jnp.where(row == tokens - 1, edge(i + 1), jnp.where(row == tokens - 2, edge(i), twice))
            total = tap(s, 0) * x
            total = total + tap(s, 1) * once
            ref[:, at] = (total + tap(s, 2) * twice).astype(BF16)
        filter_ref[:, at] = grad_filter
        for s in range(3):
            taps_out_ref[s, :, at] = edges[SUMS + 3 * s : SUMS + 3 * s + 3]
        skip_out_ref[:, at] = edges[SUMS + 9 : SUMS + 10]


def per_device(one, two, value, long_filter, short_taps, skip_gain, out_grad):
    devices = lax.axis_size("seq")
    tokens, channels = one.shape
    parts = channels // LANES
    own = LANES // devices
    anywhere = pl.BlockSpec(memory_space=pl.ANY)
    vmem = pl.BlockSpec(memory_space=pltpu.VMEM)
    smem = pl.BlockSpec(memory_space=pltpu.SMEM)
    consts = [jnp.asarray(t) for t in tables(devices, tokens, own)]
    big = (long_filter, two, value, one, out_grad, *consts)
    inward = (parts, devices, 5, own, tokens)
    outward = (parts, devices, 3, own, tokens)
    got, edges = pl.pallas_call(
        functools.partial(exchange_kernel, devices, parts, own),
        out_shape=(
            jax.ShapeDtypeStruct(outward, BF16),
            jax.ShapeDtypeStruct((devices, 1, tokens), F32),
        ),
        in_specs=[anywhere] * len(big) + [smem] * 2,
        out_specs=(anywhere, anywhere),
        scratch_shapes=[pltpu.VMEM(x.shape, x.dtype) for x in big]
        + [
            pltpu.VMEM(inward, BF16),
            pltpu.VMEM(inward, BF16),
            pltpu.VMEM(outward, BF16),
            pltpu.VMEM((devices, 1, tokens), F32),
            pltpu.SemaphoreType.DMA((len(big),)),
            pltpu.SemaphoreType.DMA((parts,)),
            pltpu.SemaphoreType.DMA((parts,)),
            pltpu.SemaphoreType.DMA((parts,)),
            pltpu.SemaphoreType.DMA((parts,)),
            pltpu.SemaphoreType.DMA((2,)),
        ],
        compiler_params=pltpu.CompilerParams(
            collective_id=0, has_side_effects=True, vmem_limit_bytes=56 * 1024 * 1024
        ),
        name="exchange",
    )(*big, short_taps, skip_gain)
    full = jax.ShapeDtypeStruct((tokens, channels), BF16)
    *outs, skip = pl.pallas_call(
        finish_kernel,
        out_shape=(
            full, full, full, full,
            jax.ShapeDtypeStruct((tokens, channels), F32),
            jax.ShapeDtypeStruct(short_taps.shape, F32),
            jax.ShapeDtypeStruct((1, channels), F32),
        ),
        in_specs=[vmem] * 7,
        out_specs=(vmem,) * 7,
        name="finish",
    )(got, edges, one, two, value, out_grad, short_taps)
    return (*outs, skip.reshape(channels))


def solution(mesh):
    rows, lanes = P("seq", "ch"), P("ch")
    taps = P(None, None, "ch")
    return jax.shard_map(
        per_device,
        mesh=mesh,
        in_specs=(rows, rows, rows, rows, taps, lanes, rows),
        out_specs=(rows, rows, rows, rows, rows, taps, lanes),
        check_vma=False,
    )
```

time: 76 us -> 53.3 us (0.70)
  local copies, waits for them, and re-layouts: 12.7 us -> 0 us
  Pallas kernels: 61.9 us -> 52.4 us
    unnamed x30 -> x0, local copies, waits for them, and re-layouts: 10.7 us -> none
    pallas_call x1, Pallas kernels: 60 us -> 50.1 us  [per_device(): pl.pallas_call(functools.partial(exchange_kernel, devices, parts, own), o...]
    reshape x2 -> x0, local copies, waits for them, and re-layouts: 2.05 us -> none  [the longest x1 1.32 us: per_device(): return (*outs, taps.reshape(3, 3, channels), skip.reshape(channels))]
where the time goes in v2:
time: 53.3 us; the launch traced here: 53.1 us
  Pallas kernels  52.4 us (98%)
  between operations  0.64 us (1%)
    pallas_call x1, Pallas kernels, per_device(): pl.pallas_call(functools.partial(exchange_kernel, devices, parts, own), o...  50.1 us
    pallas_call x1, Pallas kernels, per_device(): pl.pallas_call(finish_kernel, out_shape=(full, full, full, full, jax.Shap...  2.33 us

profile of v2, /device:TPU:24, one launch (start us, length us, event | category | flops | bytes accessed | tf_op | source)
XLA Modules:
  0.0 53.1 jit_solution(15786882401736419863)
XLA Ops:
  0.6 50.1 %exchange.1 = (bf16[2,64,3,2,128]{4,3,2,1,0:T(2,128)(2,1)}, f32[64,1,128]{2,1,0:T(1,128)}) custom-call(bf16[128,256]{1,0:T(8,128)(2,1)} %filter_in.1, bf16[128,256]{1,0:T(8,128)(2,1)} %two_ref.1, bf16[128,256]{1,0:T(8,128)(2,1)} %value_ref.1, bf16[128,256]{1,0:T(8,128)(2,1)} %one_ref.1, bf16[128,256]{1,0:T(8,128)(2,1)} %cot_ref.1, ...), custom_call_target="tpu_custom_call" | custom-call | tf_op jit(solution)/shard_map/exchange/pallas_call | solution.py:302
  50.8 2.3 %finish.1 = (bf16[128,256]{1,0:T(8,128)(2,1)}, bf16[128,256]{1,0:T(8,128)(2,1)}, bf16[128,256]{1,0:T(8,128)(2,1)}, bf16[128,256]{1,0:T(8,128)(2,1)}, f32[128,256...) custom-call(bf16[2,64,3,2,128]{4,3,2,1,0:T(2,128)(2,1)} %get-tuple-element.16.got_ref, ...), custom_call_target="tpu_custom_call" | custom-call | tf_op jit(solution)/shard_map/finish/pallas_call | solution.py:329

commit v3 on v2

v3 whole, which is shorter than its diff:
```python
import functools
import math

import jax
import jax.numpy as jnp
import numpy as np
from jax import lax
from jax.experimental import pallas as pl
from jax.experimental.pallas import tpu as pltpu
from jax.sharding import PartitionSpec as P

MESH = pl.DeviceIdType.MESH
F32 = jnp.float32
BF16 = jnp.bfloat16
LANES = 128
ROWS_Z = 16
HALO_LATER, HALO_SOONER, SUMS, FIELD = 0, 6, 12, 32


def halves(table):
    high = table.astype(BF16)
    low = (table - high.astype(np.float64)).astype(BF16)
    return high, low


def tables(devices, tokens, own):
    length = 2 * devices * tokens
    a = np.arange(devices)
    b = np.arange(tokens)
    odd = np.arange(devices) + 0.5
    outer = 2 * math.pi * np.outer(odd, a) / (2 * devices)
    first = np.concatenate([np.cos(outer), -np.sin(outer)], 0)
    last = np.concatenate([np.cos(outer.T), np.sin(outer.T)], 1) * (2.0 / length)
    turn = 2 * math.pi * np.outer(odd, b) / length
    inner = 2 * math.pi * (np.outer(b, b) % tokens) / tokens
    cosine, sine = np.cos(inner), np.sin(inner)
    second = np.block([[cosine, -sine], [sine, cosine]])
    order = np.zeros((own * devices, own * devices))
    for c in range(own):
        order[c * devices + a, a * own + c] = 1.0
    return (
        np.concatenate(halves(first), 0),
        np.stack(halves(last)),
        np.stack([np.cos(turn), -np.sin(turn)]).astype(np.float32),
        np.stack(halves(second)),
        np.stack([order, order.T]).astype(BF16),
    )


def split(x):
    high = x.astype(BF16)
    return high, (x - high.astype(F32)).astype(BF16)


def mul(a, b):
    return jnp.dot(a, b, preferred_element_type=F32)


def exchange_kernel(
    devices, parts, own, rows_z,
    filter_in, two_in, value_in, one_in, cot_in, first_in, last_in, turn_in, second_in, order_in,
    taps_in, skip_in,
    out_ref,
    filter_ref, two_ref, value_ref, one_ref, cot_ref,
    first_ref, last_ref, turn_ref, second_ref, order_ref,
    taps_ref, skip_ref,
    send, recv, ret,
    load_sem, send_sem, recv_sem, ret_sem, out_sem,
):
    me = lax.axis_index("seq")
    tokens = filter_ref.shape[0]
    rows_x = devices // rows_z
    my_x, my_z = me // rows_z, lax.rem(me, rows_z)

    columns = [lax.rem(my_x + dx, rows_x) * rows_z for dx in range(rows_x)]
    middle = rows_z // 2

    def farthest_first(visit):
        def line(dz):
            z = lax.rem(my_z + dz, rows_z)
            for column in columns:
                visit(column + z)

        def both(i, carry):
            line(middle + i)
            line(middle - i)
            return carry

        line(middle)
        lax.fori_loop(1, middle, both, 0)
        for column in columns[1:]:
            visit(column + my_z)

    barrier = pltpu.get_barrier_semaphore()
    farthest_first(
        lambda d: pl.semaphore_signal(barrier, inc=1, device_id={"seq": d}, device_id_type=MESH)
    )

    inputs = (
        filter_in, two_in, value_in, one_in, cot_in,
        first_in, last_in, turn_in, second_in, order_in, taps_in, skip_in,
    )
    held = (
        filter_ref, two_ref, value_ref, one_ref, cot_ref,
        first_ref, last_ref, turn_ref, second_ref, order_ref, taps_ref, skip_ref,
    )
    loads = [pltpu.make_async_copy(x, y, load_sem.at[i]) for i, (x, y) in enumerate(zip(inputs, held))]
    for load in loads:
        load.start()

    def spread(src, dst, at, ssem, rsem):
        def visit(d):
            pltpu.make_async_remote_copy(
                src.at[d, at], dst.at[me, at], ssem, rsem, device_id={"seq": d}, device_id_type=MESH
            ).start()

        farthest_first(visit)
        pltpu.make_async_copy(src.at[me, at], dst.at[me, at], rsem).start()

    others = pl.ds(0, devices - 1)

    def settle(ref, sem):
        pltpu.make_async_copy(ref, ref, sem).wait()

    for p in range(5):
        loads[p].wait()
        for h in range(parts):
            block = held[p][:, h * LANES : (h + 1) * LANES].T
            send[h, :, p] = block.reshape(devices, own, tokens)
    pl.semaphore_wait(barrier, devices - 1)
    inward = ((pl.ds(0, 3), pl.ds(3, 2)),) * parts
    outward = ((pl.ds(0, 3),), (pl.ds(3, 1), pl.ds(4, 3)))
    for h in range(parts):
        for i, at in enumerate(inward[h]):
            spread(send.at[h], recv.at[h], at, send_sem.at[h, i], recv_sem.at[h, i])
    for load in loads[5:]:
        load.wait()

    def sent():
        for h in range(parts):
            for i, at in enumerate(inward[h]):
                settle(send.at[h, others, at], send_sem.at[h, i])

    lane = lax.broadcasted_iota(jnp.int32, (devices, tokens), 1)
    row = lax.broadcasted_iota(jnp.int32, (devices, tokens), 0)

    def later(x, j):
        r = pltpu.roll(x, j, 1)
        up = jnp.where(row == 0, 0.0, pltpu.roll(r, 1, 0))
        return jnp.where(lane < j, up, r)

    def short(s, channel, x):
        moved = (x, later(x, 1), later(x, 2))
        total = taps_ref[s, 0, channel] * moved[0]
        total = total + taps_ref[s, 1, channel] * moved[1]
        return total + taps_ref[s, 2, channel] * moved[2], moved

    turn_re, turn_im = turn_ref[0], turn_ref[1]

    def rotate(re, im):
        return re * turn_re - im * turn_im, re * turn_im + im * turn_re

    def mul_second(x):
        high, low = split(x)
        return mul(high, second_ref[0]) + (mul(low, second_ref[0]) + mul(high, second_ref[1]))

    def rows_of(x, i):
        return x[i * devices : (i + 1) * devices]

    def forward(pieces):
        rows = []
        for x in pieces:
            both = mul(first_ref[...], x)
            both = both[: 2 * devices] + both[2 * devices :]
            rows.append(jnp.concatenate(rotate(both[:devices], both[devices:]), 1))
        full = mul_second(jnp.concatenate(rows, 0))
        size = own * devices
        return [
            (full[i * size : (i + 1) * size, :tokens], full[i * size : (i + 1) * size, tokens:])
            for i in range(len(pieces) // own)
        ]

    def inverse(spectra):
        full = mul_second(jnp.concatenate([jnp.concatenate(z, 1) for z in spectra], 0))
        result = []
        for i in range(len(spectra) * own):
            part = rows_of(full, i)
            high, low = split(jnp.concatenate(rotate(part[:, :tokens], part[:, tokens:]), 0))
            result.append(mul(last_ref[0], high) + (mul(last_ref[0], low) + mul(last_ref[1], high)))
        return [result[i * own : (i + 1) * own] for i in range(len(spectra))]

    ones = jnp.ones((tokens, tokens), BF16)

    def gather(h, p):
        x = mul(order_ref[0], recv[h, :, p].reshape(devices * own, tokens))
        return [rows_of(x, c) for c in range(own)]

    def give(p, pieces):
        stacked = jnp.concatenate([x.astype(BF16) for x in pieces], 0)
        ret[:, p] = mul(order_ref[1], stacked).astype(BF16).reshape(devices, own, tokens)

    each = range(own)
    edges = jnp.zeros((devices, tokens), F32)
    for h in range(parts):
        channels = [h * LANES + own * me + c for c in each]
        skip = [skip_ref[channels[c]] for c in each]
        settle(recv.at[h, :, inward[h][0]], recv_sem.at[h, 0])
        filt = [x.astype(BF16) for x in gather(h, 0)]
        two = [short(1, channels[c], x) for c, x in enumerate(gather(h, 1))]
        val = [short(2, channels[c], x) for c, x in enumerate(gather(h, 2))]
        mixed = [(two[c][0] * val[c][0]).astype(BF16) for c in each]
        (f_re, f_im), (m_re, m_im) = forward(filt + mixed)
        (conv,) = inverse([(m_re * f_re - m_im * f_im, -(m_re * f_im + m_im * f_re))])
        mixed_wide = [x.astype(F32) for x in mixed]
        long_out = [conv[c] + skip[c] * mixed_wide[c] for c in each]
        give(3 * h, long_out)
        if h == parts - 1:
            spread(ret, out_ref, outward[h][0], ret_sem.at[h, 0], out_sem.at[h, 0])

        settle(recv.at[h, :, inward[h][1]], recv_sem.at[h, 1])
        one = [short(0, channels[c], x) for c, x in enumerate(gather(h, 3))]
        cot = gather(h, 4)
        back = [(cot[c] * one[c][0]).astype(BF16) for c in each]
        ((b_re, b_im),) = forward(back)
        grad_mixed, grad_filter = inverse([
            (b_re * f_re + b_im * f_im, b_re * f_im - b_im * f_re),
            (b_re * m_re + b_im * m_im, b_re * m_im - b_im * m_re),
        ])
        back_wide = [x.astype(F32) for x in back]
        grad_in = [grad_mixed[c] + skip[c] * back_wide[c] for c in each]
        give(3 * h + 1, grad_in)
        give(3 * h + 2, grad_filter)
        if h < parts - 1:
            sent()
            spread(ret, out_ref, outward[h][0], ret_sem.at[h, 0], out_sem.at[h, 0])
        sections = []
        for c in each:
            field = FIELD * (own * h + c)
            grads = (cot[c] * long_out[c], grad_in[c] * val[c][0], grad_in[c] * two[c][0])
            streams = (one[c][1], two[c][1], val[c][1])
            for s in range(3):
                at = field + HALO_LATER + 2 * s
                piece = pltpu.roll(streams[s][2], at, 1) if at else streams[s][2]
                edges = jnp.where((lane >= at) & (lane < at + 2), piece, edges)
                at = field + HALO_SOONER + 2 * s
                ahead = jnp.where(row == devices - 1, 0.0, pltpu.roll(grads[s], devices - 1, 0))
                edges = jnp.where((lane >= at) & (lane < at + 2), pltpu.roll(ahead, at, 1), edges)
                for j in range(3):
                    sections.append(grads[s] * streams[s][j])
            sections.append(back_wide[c] * mixed_wide[c])
            sections += [None] * 6
        gathered = [
            jnp.zeros((8, tokens), F32) if x is None else x.reshape(devices // 8, 8, tokens).sum(0)
            for x in sections
        ]
        high, low = split(jnp.concatenate(gathered, 0))
        totals = mul(high, ones) + mul(low, ones)
        section = lax.broadcasted_iota(jnp.int32, totals.shape, 0) // 8
        target = FIELD * (own * h + section // 16) + SUMS + section % 16
        pick = lax.broadcasted_iota(jnp.int32, totals.shape, 1) == target
        edges = edges + jnp.where(pick, totals, 0.0).sum(0, keepdims=True)
    give(3 * parts, split(edges))
    spread(ret, out_ref, outward[-1][1], ret_sem.at[parts - 1, 1], out_sem.at[parts - 1, 1])

    for h in range(parts):
        for i, at in enumerate(outward[h]):
            settle(ret.at[others, at], ret_sem.at[h, i])
            settle(out_ref.at[:, at], out_sem.at[h, i])


def finish_kernel(
    got_ref, one_ref, two_ref, value_ref, cot_ref, taps_ref,
    mixed_out_ref, grad_one_ref, grad_two_ref, grad_value_ref, filter_ref, taps_out_ref, skip_out_ref,
):
    devices, units, own, tokens = got_ref.shape
    parts = units // 3
    source = lax.broadcasted_iota(jnp.int32, (LANES, LANES), 0)
    target = lax.broadcasted_iota(jnp.int32, (LANES, LANES), 1)
    row = lax.broadcasted_iota(jnp.int32, (tokens, LANES), 0)

    def turn(p):
        return got_ref[:, p].reshape(LANES, tokens).T

    turned = turn(3 * parts)
    for h in range(parts):
        at = slice(h * LANES, (h + 1) * LANES)
        long_out, grad_in, grad_filter = [turn(3 * h + p) for p in range(3)]
        long_out, grad_in = long_out.astype(F32), grad_in.astype(F32)
        edges = jnp.zeros((FIELD, LANES), F32)
        for c in range(own):
            place = jnp.where((source // own == target // own) & (target % own == c), 1.0, 0.0)
            field = FIELD * (own * h + c)
            edges = edges + mul(turned[field : field + FIELD], place.astype(BF16))

        def edge(i):
            return edges[i : i + 1]

        def tap(s, j):
            return taps_ref[s, j : j + 1, at]

        gates = []
        for s, ref in enumerate((one_ref, two_ref, value_ref)):
            x = ref[:, at].astype(F32)
            i = HALO_LATER + 2 * s
            once = jnp.where(row == 0, edge(i + 1), pltpu.roll(x, 1, 0))
            twice = jnp.where(row == 0, edge(i), jnp.where(row == 1, edge(i + 1), pltpu.roll(x, 2, 0)))
            total = tap(s, 0) * x
            total = total + tap(s, 1) * once
            gates.append(total + tap(s, 2) * twice)
        mixed_out_ref[:, at] = (gates[0] * long_out).astype(BF16)
        grads = (cot_ref[:, at].astype(F32) * long_out, grad_in * gates[2], grad_in * gates[1])
        for s, ref in enumerate((grad_one_ref, grad_two_ref, grad_value_ref)):
            x = grads[s]
            i = HALO_SOONER + 2 * s
            once = jnp.where(row == tokens - 1, edge(i), pltpu.roll(x, tokens - 1, 0))
            twice = pltpu.roll(x, tokens - 2, 0)
            twice = jnp.where(row == tokens - 1, edge(i + 1), jnp.where(row == tokens - 2, edge(i), twice))
            total = tap(s, 0) * x
            total = total + tap(s, 1) * once
            ref[:, at] = (total + tap(s, 2) * twice).astype(BF16)
        filter_ref[:, at] = grad_filter.astype(F32)
        for s in range(3):
            taps_out_ref[s, :, at] = edges[SUMS + 3 * s : SUMS + 3 * s + 3]
        skip_out_ref[:, at] = edges[SUMS + 9 : SUMS + 10]


def per_device(rows_z, one, two, value, long_filter, short_taps, skip_gain, out_grad):
    devices = lax.axis_size("seq")
    tokens, channels = one.shape
    parts = channels // LANES
    own = LANES // devices
    anywhere = pl.BlockSpec(memory_space=pl.ANY)
    vmem = pl.BlockSpec(memory_space=pltpu.VMEM)
    consts = [jnp.asarray(t) for t in tables(devices, tokens, own)]
    big = (long_filter, two, value, one, out_grad, *consts)
    inward = (parts, devices, 5, own, tokens)
    outward = (devices, 3 * parts + 1, own, tokens)
    got = pl.pallas_call(
        functools.partial(exchange_kernel, devices, parts, own, rows_z),
        out_shape=jax.ShapeDtypeStruct(outward, BF16),
        in_specs=[anywhere] * (len(big) + 2),
        out_specs=anywhere,
        scratch_shapes=[pltpu.VMEM(x.shape, x.dtype) for x in big]
        + [
            pltpu.SMEM(short_taps.shape, F32),
            pltpu.SMEM(skip_gain.shape, F32),
            pltpu.VMEM(inward, BF16),
            pltpu.VMEM(inward, BF16),
            pltpu.VMEM(outward, BF16),
            pltpu.SemaphoreType.DMA((len(big) + 2,)),
            pltpu.SemaphoreType.DMA((parts, 2)),
            pltpu.SemaphoreType.DMA((parts, 2)),
            pltpu.SemaphoreType.DMA((parts, 2)),
            pltpu.SemaphoreType.DMA((parts, 2)),
        ],
        compiler_params=pltpu.CompilerParams(
            collective_id=0, has_side_effects=True, vmem_limit_bytes=56 * 1024 * 1024
        ),
        name="exchange",
    )(*big, short_taps, skip_gain)
    full = jax.ShapeDtypeStruct((tokens, channels), BF16)
    *outs, skip = pl.pallas_call(
        finish_kernel,
        out_shape=(
            full, full, full, full,
            jax.ShapeDtypeStruct((tokens, channels), F32),
            jax.ShapeDtypeStruct(short_taps.shape, F32),
            jax.ShapeDtypeStruct((1, channels), F32),
        ),
        in_specs=[vmem] * 6,
        out_specs=(vmem,) * 7,
        name="finish",
    )(got, one, two, value, out_grad, short_taps)
    return (*outs, skip.reshape(channels))


def solution(mesh):
    rows, lanes = P("seq", "ch"), P("ch")
    taps = P(None, None, "ch")
    return jax.shard_map(
        functools.partial(per_device, ROWS_Z),
        mesh=mesh,
        in_specs=(rows, rows, rows, rows, taps, lanes, rows),
        out_specs=(rows, rows, rows, rows, rows, taps, lanes),
        check_vma=False,
    )
```

time: 53.3 us -> 49.5 us (0.929)
  Pallas kernels: 52.4 us -> 48.7 us
    pallas_call x1, Pallas kernels: 50.1 us -> 46.5 us  [per_device(): pl.pallas_call(functools.partial(exchange_kernel, devices, parts, own, ro...]
where the time goes in v3:
time: 49.5 us; the launch traced here: 49.4 us
  Pallas kernels  48.7 us (98%)
  between operations  0.64 us (1%)
    pallas_call x1, Pallas kernels, per_device(): pl.pallas_call(functools.partial(exchange_kernel, devices, parts, own, ro...  46.5 us
    pallas_call x1, Pallas kernels, per_device(): pl.pallas_call(finish_kernel, out_shape=(full, full, full, full, jax.Shap...  2.23 us

profile of v3, /device:TPU:24, one launch (start us, length us, event | category | flops | bytes accessed | tf_op | source)
XLA Modules:
  0.0 49.4 jit_solution(14592510593625502559)
XLA Ops:
  0.6 46.5 %exchange.1.got_ref = bf16[64,7,2,128]{3,2,1,0:T(2,128)(2,1)} custom-call(bf16[128,256]{1,0:T(8,128)(2,1)} %filter_in.1, bf16[128,256]{1,0:T(8,128)(2,1)} %two_ref.1, bf16[128,256]{1,0:T(8,128)(2,1)} %value_ref.1, bf16[128,256]{1,0:T(8,128)(2,1)} %one_ref.1, bf16[128,256]{1,0:T(8,128)(2,1)} %cot_ref.1, bf16[256,64]{1,0:T(8,128)(2,1)} %constant.10.clone.first_in, ...), custom_call_target="tpu_custom_call" | custom-call | tf_op jit(solution)/shard_map/exchange/pallas_call | solution.py:338
  47.1 2.2 %finish.1 = (bf16[128,256]{1,0:T(8,128)(2,1)}, bf16[128,256]{1,0:T(8,128)(2,1)}, bf16[128,256]{1,0:T(8,128)(2,1)}, bf16[128,256]{1,0:T(8,128)(2,1)}, f32[128,256...) custom-call(bf16[64,7,2,128]{3,2,1,0:T(2,128)(2,1)} %exchange.1.got_ref, bf16[128,256]{1,0:T(8,128)(2,1)} %one_ref.1, ...), custom_call_target="tpu_custom_call" | custom-call | tf_op jit(solution)/shard_map/finish/pallas_call | solution.py:362

commit v4 on v3

--- a/solution.py
+++ b/solution.py
@@ -128,18 +128,15 @@
             block = held[p][:, h * LANES : (h + 1) * LANES].T
             send[h, :, p] = block.reshape(devices, own, tokens)
     pl.semaphore_wait(barrier, devices - 1)
-    inward = ((pl.ds(0, 3), pl.ds(3, 2)),) * parts
-    outward = ((pl.ds(0, 3),), (pl.ds(3, 1), pl.ds(4, 3)))
+    outward = (pl.ds(0, 3), pl.ds(3, 4))
     for h in range(parts):
-        for i, at in enumerate(inward[h]):
-            spread(send.at[h], recv.at[h], at, send_sem.at[h, i], recv_sem.at[h, i])
+        spread(send.at[h], recv.at[h], pl.ds(0, 5), send_sem.at[h], recv_sem.at[h])
     for load in loads[5:]:
         load.wait()
 
     def sent():
         for h in range(parts):
-            for i, at in enumerate(inward[h]):
-                settle(send.at[h, others, at], send_sem.at[h, i])
+            settle(send.at[h, others], send_sem.at[h])
 
     lane = lax.broadcasted_iota(jnp.int32, (devices, tokens), 1)
     row = lax.broadcasted_iota(jnp.int32, (devices, tokens), 0)
@@ -204,35 +201,30 @@
     for h in range(parts):
         channels = [h * LANES + own * me + c for c in each]
         skip = [skip_ref[channels[c]] for c in each]
-        settle(recv.at[h, :, inward[h][0]], recv_sem.at[h, 0])
+        settle(recv.at[h], recv_sem.at[h])
         filt = [x.astype(BF16) for x in gather(h, 0)]
         two = [short(1, channels[c], x) for c, x in enumerate(gather(h, 1))]
         val = [short(2, channels[c], x) for c, x in enumerate(gather(h, 2))]
+        one = [short(0, channels[c], x) for c, x in enumerate(gather(h, 3))]
+        cot = gather(h, 4)
         mixed = [(two[c][0] * val[c][0]).astype(BF16) for c in each]
-        (f_re, f_im), (m_re, m_im) = forward(filt + mixed)
-        (conv,) = inverse([(m_re * f_re - m_im * f_im, -(m_re * f_im + m_im * f_re))])
+        back = [(cot[c] * one[c][0]).astype(BF16) for c in each]
+        (f_re, f_im), (m_re, m_im), (b_re, b_im) = forward(filt + mixed + back)
+        conv, grad_mixed, grad_filter = inverse([
+            (m_re * f_re - m_im * f_im, -(m_re * f_im + m_im * f_re)),
+            (b_re * f_re + b_im * f_im, b_re * f_im - b_im * f_re),
+            (b_re * m_re + b_im * m_im, b_re * m_im - b_im * m_re),
+        ])
         mixed_wide = [x.astype(F32) for x in mixed]
         long_out = [conv[c] + skip[c] * mixed_wide[c] for c in each]
         give(3 * h, long_out)
-        if h == parts - 1:
-            spread(ret, out_ref, outward[h][0], ret_sem.at[h, 0], out_sem.at[h, 0])
-
-        settle(recv.at[h, :, inward[h][1]], recv_sem.at[h, 1])
-        one = [short(0, channels[c], x) for c, x in enumerate(gather(h, 3))]
-        cot = gather(h, 4)
-        back = [(cot[c] * one[c][0]).astype(BF16) for c in each]
-        ((b_re, b_im),) = forward(back)
-        grad_mixed, grad_filter = inverse([
-            (b_re * f_re + b_im * f_im, b_re * f_im - b_im * f_re),
-            (b_re * m_re + b_im * m_im, b_re * m_im - b_im * m_re),
-        ])
         back_wide = [x.astype(F32) for x in back]
         grad_in = [grad_mixed[c] + skip[c] * back_wide[c] for c in each]
         give(3 * h + 1, grad_in)
         give(3 * h + 2, grad_filter)
         if h < parts - 1:
             sent()
-            spread(ret, out_ref, outward[h][0], ret_sem.at[h, 0], out_sem.at[h, 0])
+            spread(ret, out_ref, outward[h], ret_sem.at[h], out_sem.at[h])
         sections = []
         for c in each:
             field = FIELD * (own * h + c)
@@ -260,12 +252,11 @@
         pick = lax.broadcasted_iota(jnp.int32, totals.shape, 1) == target
         edges = edges + jnp.where(pick, totals, 0.0).sum(0, keepdims=True)
     give(3 * parts, split(edges))
-    spread(ret, out_ref, outward[-1][1], ret_sem.at[parts - 1, 1], out_sem.at[parts - 1, 1])
+    spread(ret, out_ref, outward[-1], ret_sem.at[parts - 1], out_sem.at[parts - 1])
 
     for h in range(parts):
-        for i, at in enumerate(outward[h]):
-            settle(ret.at[others, at], ret_sem.at[h, i])
-            settle(out_ref.at[:, at], out_sem.at[h, i])
+        settle(ret.at[others, outward[h]], ret_sem.at[h])
+        settle(out_ref.at[:, outward[h]], out_sem.at[h])
 
 
 def finish_kernel(
@@ -348,10 +339,10 @@
             pltpu.VMEM(inward, BF16),
             pltpu.VMEM(outward, BF16),
             pltpu.SemaphoreType.DMA((len(big) + 2,)),
-            pltpu.SemaphoreType.DMA((parts, 2)),
-            pltpu.SemaphoreType.DMA((parts, 2)),
-            pltpu.SemaphoreType.DMA((parts, 2)),
-            pltpu.SemaphoreType.DMA((parts, 2)),
+            pltpu.SemaphoreType.DMA((parts,)),
+            pltpu.SemaphoreType.DMA((parts,)),
+            pltpu.SemaphoreType.DMA((parts,)),
+            pltpu.SemaphoreType.DMA((parts,)),
         ],
         compiler_params=pltpu.CompilerParams(
             collective_id=0, has_side_effects=True, vmem_limit_bytes=56 * 1024 * 1024

time: 49.5 us -> 48.7 us (0.984)
  Pallas kernels: 48.7 us -> 47.9 us
    pallas_call x1, Pallas kernels: 46.5 us -> 45.7 us  [per_device(): pl.pallas_call(functools.partial(exchange_kernel, devices, parts, own, ro...]
where the time goes in v4:
time: 48.7 us; the launch traced here: 48.6 us
  Pallas kernels  47.9 us (98%)
  between operations  0.64 us (1%)
    pallas_call x1, Pallas kernels, per_device(): pl.pallas_call(functools.partial(exchange_kernel, devices, parts, own, ro...  45.7 us
    pallas_call x1, Pallas kernels, per_device(): pl.pallas_call(finish_kernel, out_shape=(full, full, full, full, jax.Shap...  2.23 us

profile of v4, /device:TPU:24, one launch (start us, length us, event | category | flops | bytes accessed | tf_op | source)
XLA Modules:
  0.0 48.6 jit_solution(18327632117986113762)
XLA Ops:
  0.6 45.7 %exchange.1.got_ref = bf16[64,7,2,128]{3,2,1,0:T(2,128)(2,1)} custom-call(bf16[128,256]{1,0:T(8,128)(2,1)} %filter_in.1, bf16[128,256]{1,0:T(8,128)(2,1)} %two_ref.1, bf16[128,256]{1,0:T(8,128)(2,1)} %value_ref.1, bf16[128,256]{1,0:T(8,128)(2,1)} %one_ref.1, bf16[128,256]{1,0:T(8,128)(2,1)} %cot_ref.1, bf16[256,64]{1,0:T(8,128)(2,1)} %constant.10.clone.first_in, ...), custom_call_target="tpu_custom_call" | custom-call | tf_op jit(solution)/shard_map/exchange/pallas_call | solution.py:329
  46.3 2.2 %finish.1 = (bf16[128,256]{1,0:T(8,128)(2,1)}, bf16[128,256]{1,0:T(8,128)(2,1)}, bf16[128,256]{1,0:T(8,128)(2,1)}, bf16[128,256]{1,0:T(8,128)(2,1)}, f32[128,256...) custom-call(bf16[64,7,2,128]{3,2,1,0:T(2,128)(2,1)} %exchange.1.got_ref, bf16[128,256]{1,0:T(8,128)(2,1)} %one_ref.1, ...), custom_call_target="tpu_custom_call" | custom-call | tf_op jit(solution)/shard_map/finish/pallas_call | solution.py:353

commit v5 on v4

--- a/solution.py
+++ b/solution.py
@@ -72,7 +72,7 @@
     rows_x = devices // rows_z
     my_x, my_z = me // rows_z, lax.rem(me, rows_z)
 
-    columns = [lax.rem(my_x + dx, rows_x) * rows_z for dx in range(rows_x)]
+    columns = [lax.rem(my_x + dx, rows_x) * rows_z for dx in (2, 1, 3, 0)]
     middle = rows_z // 2
 
     def farthest_first(visit):
@@ -88,7 +88,7 @@
 
         line(middle)
         lax.fori_loop(1, middle, both, 0)
-        for column in columns[1:]:
+        for column in columns[:-1]:
             visit(column + my_z)
 
     barrier = pltpu.get_barrier_semaphore()

time: 48.7 us -> 48.5 us (level)
  no operation moved by 1% of the time
where the time goes in v5:
time: 48.5 us; the launch traced here: 48.3 us
  Pallas kernels  47.7 us (98%)
  between operations  0.64 us (1%)
    pallas_call x1, Pallas kernels, per_device(): pl.pallas_call(functools.partial(exchange_kernel, devices, parts, own, ro...  45.5 us
    pallas_call x1, Pallas kernels, per_device(): pl.pallas_call(finish_kernel, out_shape=(full, full, full, full, jax.Shap...  2.23 us

profile of v5, /device:TPU:24, one launch (start us, length us, event | category | flops | bytes accessed | tf_op | source)
XLA Modules:
  0.0 48.3 jit_solution(9357420158587924027)
XLA Ops:
  0.6 45.5 %exchange.1.got_ref = bf16[64,7,2,128]{3,2,1,0:T(2,128)(2,1)} custom-call(bf16[128,256]{1,0:T(8,128)(2,1)} %filter_in.1, bf16[128,256]{1,0:T(8,128)(2,1)} %two_ref.1, bf16[128,256]{1,0:T(8,128)(2,1)} %value_ref.1, bf16[128,256]{1,0:T(8,128)(2,1)} %one_ref.1, bf16[128,256]{1,0:T(8,128)(2,1)} %cot_ref.1, bf16[256,64]{1,0:T(8,128)(2,1)} %constant.10.clone.first_in, ...), custom_call_target="tpu_custom_call" | custom-call | tf_op jit(solution)/shard_map/exchange/pallas_call | solution.py:329
  46.1 2.2 %finish.1 = (bf16[128,256]{1,0:T(8,128)(2,1)}, bf16[128,256]{1,0:T(8,128)(2,1)}, bf16[128,256]{1,0:T(8,128)(2,1)}, bf16[128,256]{1,0:T(8,128)(2,1)}, f32[128,256...) custom-call(bf16[64,7,2,128]{3,2,1,0:T(2,128)(2,1)} %exchange.1.got_ref, bf16[128,256]{1,0:T(8,128)(2,1)} %one_ref.1, ...), custom_call_target="tpu_custom_call" | custom-call | tf_op jit(solution)/shard_map/finish/pallas_call | solution.py:353

commit v6 on v5

--- a/solution.py
+++ b/solution.py
@@ -126,17 +126,18 @@
         loads[p].wait()
         for h in range(parts):
             block = held[p][:, h * LANES : (h + 1) * LANES].T
-            send[h, :, p] = block.reshape(devices, own, tokens)
+            send[:, 5 * h + p] = block.reshape(devices, own, tokens)
     pl.semaphore_wait(barrier, devices - 1)
+    forth = (pl.ds(0, 6), pl.ds(6, 4))
     outward = (pl.ds(0, 3), pl.ds(3, 4))
     for h in range(parts):
-        spread(send.at[h], recv.at[h], pl.ds(0, 5), send_sem.at[h], recv_sem.at[h])
+        spread(send, recv, forth[h], send_sem.at[h], recv_sem.at[h])
     for load in loads[5:]:
         load.wait()
 
     def sent():
         for h in range(parts):
-            settle(send.at[h, others], send_sem.at[h])
+            settle(send.at[others, forth[h]], send_sem.at[h])
 
     lane = lax.broadcasted_iota(jnp.int32, (devices, tokens), 1)
     row = lax.broadcasted_iota(jnp.int32, (devices, tokens), 0)
@@ -189,7 +190,7 @@
     ones = jnp.ones((tokens, tokens), BF16)
 
     def gather(h, p):
-        x = mul(order_ref[0], recv[h, :, p].reshape(devices * own, tokens))
+        x = mul(order_ref[0], recv[:, 5 * h + p].reshape(devices * own, tokens))
         return [rows_of(x, c) for c in range(own)]
 
     def give(p, pieces):
@@ -197,19 +198,22 @@
         ret[:, p] = mul(order_ref[1], stacked).astype(BF16).reshape(devices, own, tokens)
 
     each = range(own)
+    filters = []
     edges = jnp.zeros((devices, tokens), F32)
     for h in range(parts):
         channels = [h * LANES + own * me + c for c in each]
         skip = [skip_ref[channels[c]] for c in each]
-        settle(recv.at[h], recv_sem.at[h])
-        filt = [x.astype(BF16) for x in gather(h, 0)]
+        settle(recv.at[:, forth[h]], recv_sem.at[h])
+        fresh = [x.astype(BF16) for k in ((0, 1) if h == 0 else ()) for x in gather(k, 0)]
         two = [short(1, channels[c], x) for c, x in enumerate(gather(h, 1))]
         val = [short(2, channels[c], x) for c, x in enumerate(gather(h, 2))]
         one = [short(0, channels[c], x) for c, x in enumerate(gather(h, 3))]
         cot = gather(h, 4)
         mixed = [(two[c][0] * val[c][0]).astype(BF16) for c in each]
         back = [(cot[c] * one[c][0]).astype(BF16) for c in each]
-        (f_re, f_im), (m_re, m_im), (b_re, b_im) = forward(filt + mixed + back)
+        (m_re, m_im), (b_re, b_im), *more = forward(mixed + back + fresh)
+        filters += more
+        f_re, f_im = filters[h]
         conv, grad_mixed, grad_filter = inverse([
             (m_re * f_re - m_im * f_im, -(m_re * f_im + m_im * f_re)),
             (b_re * f_re + b_im * f_im, b_re * f_im - b_im * f_re),
@@ -324,7 +328,7 @@
     vmem = pl.BlockSpec(memory_space=pltpu.VMEM)
     consts = [jnp.asarray(t) for t in tables(devices, tokens, own)]
     big = (long_filter, two, value, one, out_grad, *consts)
-    inward = (parts, devices, 5, own, tokens)
+    inward = (devices, 5 * parts, own, tokens)
     outward = (devices, 3 * parts + 1, own, tokens)
     got = pl.pallas_call(
         functools.partial(exchange_kernel, devices, parts, own, rows_z),

time: 48.5 us -> 48.4 us (level)
  no operation moved by 1% of the time
where the time goes in v6:
time: 48.4 us; the launch traced here: 48.2 us
  Pallas kernels  47.6 us (98%)
  between operations  0.64 us (1%)
    pallas_call x1, Pallas kernels, per_device(): pl.pallas_call(functools.partial(exchange_kernel, devices, parts, own, ro...  45.4 us
    pallas_call x1, Pallas kernels, per_device(): pl.pallas_call(finish_kernel, out_shape=(full, full, full, full, jax.Shap...  2.23 us

profile of v6, /device:TPU:24, one launch (start us, length us, event | category | flops | bytes accessed | tf_op | source)
XLA Modules:
  0.0 48.2 jit_solution(2930364882609772125)
XLA Ops:
  0.6 45.4 %exchange.1.got_ref = bf16[64,7,2,128]{3,2,1,0:T(2,128)(2,1)} custom-call(bf16[128,256]{1,0:T(8,128)(2,1)} %filter_in.1, bf16[128,256]{1,0:T(8,128)(2,1)} %two_ref.1, bf16[128,256]{1,0:T(8,128)(2,1)} %value_ref.1, bf16[128,256]{1,0:T(8,128)(2,1)} %one_ref.1, bf16[128,256]{1,0:T(8,128)(2,1)} %cot_ref.1, bf16[256,64]{1,0:T(8,128)(2,1)} %constant.10.clone.first_in, ...), custom_call_target="tpu_custom_call" | custom-call | tf_op jit(solution)/shard_map/exchange/pallas_call | solution.py:333
  46.0 2.2 %finish.1 = (bf16[128,256]{1,0:T(8,128)(2,1)}, bf16[128,256]{1,0:T(8,128)(2,1)}, bf16[128,256]{1,0:T(8,128)(2,1)}, bf16[128,256]{1,0:T(8,128)(2,1)}, f32[128,256...) custom-call(bf16[64,7,2,128]{3,2,1,0:T(2,128)(2,1)} %exchange.1.got_ref, bf16[128,256]{1,0:T(8,128)(2,1)} %one_ref.1, ...), custom_call_target="tpu_custom_call" | custom-call | tf_op jit(solution)/shard_map/finish/pallas_call | solution.py:357

commit v7 on v6

--- a/solution.py
+++ b/solution.py
@@ -227,7 +227,6 @@
         give(3 * h + 1, grad_in)
         give(3 * h + 2, grad_filter)
         if h < parts - 1:
-            sent()
             spread(ret, out_ref, outward[h], ret_sem.at[h], out_sem.at[h])
         sections = []
         for c in each:
@@ -258,6 +257,7 @@
     give(3 * parts, split(edges))
     spread(ret, out_ref, outward[-1], ret_sem.at[parts - 1], out_sem.at[parts - 1])
 
+    sent()
     for h in range(parts):
         settle(ret.at[others, outward[h]], ret_sem.at[h])
         settle(out_ref.at[:, outward[h]], out_sem.at[h])

time: 48.4 us -> 48.7 us (level)
  no operation moved by 1% of the time
where the time goes in v7:
time: 48.7 us; the launch traced here: 48.5 us
  Pallas kernels  47.9 us (98%)
  between operations  0.64 us (1%)
    pallas_call x1, Pallas kernels, per_device(): pl.pallas_call(functools.partial(exchange_kernel, devices, parts, own, ro...  45.7 us
    pallas_call x1, Pallas kernels, per_device(): pl.pallas_call(finish_kernel, out_shape=(full, full, full, full, jax.Shap...  2.23 us

profile of v7, /device:TPU:24, one launch (start us, length us, event | category | flops | bytes accessed | tf_op | source)
XLA Modules:
  0.0 48.5 jit_solution(14116045192592376112)
XLA Ops:
  0.6 45.7 %exchange.1.got_ref = bf16[64,7,2,128]{3,2,1,0:T(2,128)(2,1)} custom-call(bf16[128,256]{1,0:T(8,128)(2,1)} %filter_in.1, bf16[128,256]{1,0:T(8,128)(2,1)} %two_ref.1, bf16[128,256]{1,0:T(8,128)(2,1)} %value_ref.1, bf16[128,256]{1,0:T(8,128)(2,1)} %one_ref.1, bf16[128,256]{1,0:T(8,128)(2,1)} %cot_ref.1, bf16[256,64]{1,0:T(8,128)(2,1)} %constant.10.clone.first_in, ...), custom_call_target="tpu_custom_call" | custom-call | tf_op jit(solution)/shard_map/exchange/pallas_call | solution.py:333
  46.3 2.2 %finish.1 = (bf16[128,256]{1,0:T(8,128)(2,1)}, bf16[128,256]{1,0:T(8,128)(2,1)}, bf16[128,256]{1,0:T(8,128)(2,1)}, bf16[128,256]{1,0:T(8,128)(2,1)}, f32[128,256...) custom-call(bf16[64,7,2,128]{3,2,1,0:T(2,128)(2,1)} %exchange.1.got_ref, bf16[128,256]{1,0:T(8,128)(2,1)} %one_ref.1, ...), custom_call_target="tpu_custom_call" | custom-call | tf_op jit(solution)/shard_map/finish/pallas_call | solution.py:357
